TPU v7x, 256 devices: a whole 4x4x8 slice. The times are simulated.
256 devices in a mesh: tx: 128 (over x_lo, z, y, core), ty: 2 (over x_hi).
Axes of the slice: x: 4 (x_hi: 2, x_lo: 2; x = x_hi * 2 + x_lo), y: 4, z: 8, core: 2. Of those that a mesh axis runs over, the one named last changes fastest.
Arguments:
- obj_re: float32 [65536, 512], P('tx', 'ty')
- obj_im: float32 [65536, 512], P('tx', 'ty')
- probe_re: float32 [256, 256], replicated, may hold values from -6 to 6
- probe_im: float32 [256, 256], replicated, may hold values from -6 to 6
- amplitude: float32 [128, 2, 12, 256, 256], P('tx', 'ty'), may hold values from 0 to 2
- offsets: int32 [128, 2, 12, 2], P('tx'), may hold values from 0 to 65280, as said below
- counts: int32 [128, 2], P('tx'), may hold values from 3 to 12, as said below
Outputs:
- grad_obj_re: float32 [65536, 512], P('tx', 'ty')
- grad_obj_im: float32 [65536, 512], P('tx', 'ty')
- grad_probe_re: float32 [256, 256], replicated
- grad_probe_im: float32 [256, 256], replicated
Inputs may be any that keep to these rules, and one draw needn't show every extreme that they name: Tile (a, b)'s slots hold positions whose top-left row lies in rows a * 512 to (a + 1) * 512 - 1 and whose centre column lies in columns b * 256 to (b + 1) * 256 - 1; every window lies inside the object. Slots at or beyond the tile's count hold such offsets too. `counts`: live positions per tile.
All inputs are finite; a program needn't handle non-finite values.
Results may differ from a plain program's by a relative error of at most 0.0001.
Values sent between devices are 32-bit elements; how exact they have to be, the bound alone decides.
A program may use at most 64 MiB of HBM per device.

v0:
```python
import math

import jax
import jax.numpy as jnp
from jax import lax
from jax.sharding import PartitionSpec as P


def passed_along(value, axis, steps):
    count = lax.axis_size(axis)
    initial, last = (max(0, -steps), min(count, count - steps))
    return lax.ppermute(value, axis, [(source, source + steps) for source in range(initial, last)])


def make_tables(length):
    ids = jnp.arange(length, dtype=jnp.int32)
    product = ids[:, None] * ids[None, :] % length
    angle = product.astype(jnp.float32) * (2.0 * math.pi / length)
    factor = 1.0 / math.sqrt(length)
    return (jnp.cos(angle) * factor, jnp.sin(angle) * factor)


def matmul(left, right):
    return jnp.dot(left, right, precision=lax.Precision.HIGHEST, preferred_element_type=jnp.float32)


def one_position(
    totals, region_re, region_im, probe_re, probe_im, cosine, sine_table, measured, row_at, col_at
):
    grad_re, grad_im, pgrad_re, pgrad_im = totals
    patch_size = probe_re.shape[0]
    piece_re = lax.dynamic_slice(region_re, (row_at, col_at), (patch_size, patch_size))
    piece_im = lax.dynamic_slice(region_im, (row_at, col_at), (patch_size, patch_size))
    exit_re = probe_re * piece_re - probe_im * piece_im
    exit_im = probe_re * piece_im + probe_im * piece_re
    left_re = matmul(cosine, exit_re) + matmul(sine_table, exit_im)
    left_im = matmul(cosine, exit_im) - matmul(sine_table, exit_re)
    far_re = matmul(left_re, cosine) + matmul(left_im, sine_table)
    far_im = matmul(left_im, cosine) - matmul(left_re, sine_table)
    modulus = jnp.sqrt(far_re * far_re + far_im * far_im)
    keep_part = 1.0 - measured / jnp.maximum(modulus, 1.0)
    diff_re = far_re * keep_part
    diff_im = far_im * keep_part
    back_re = matmul(cosine, diff_re) - matmul(sine_table, diff_im)
    back_im = matmul(cosine, diff_im) + matmul(sine_table, diff_re)
    chi_re = matmul(back_re, cosine) - matmul(back_im, sine_table)
    chi_im = matmul(back_im, cosine) + matmul(back_re, sine_table)
    now_re = lax.dynamic_slice(grad_re, (row_at, col_at), (patch_size, patch_size))
    now_im = lax.dynamic_slice(grad_im, (row_at, col_at), (patch_size, patch_size))
    grad_re = lax.dynamic_update_slice(
        grad_re, now_re + probe_re * chi_re + probe_im * chi_im, (row_at, col_at)
    )
    grad_im = lax.dynamic_update_slice(
        grad_im, now_im + probe_re * chi_im - probe_im * chi_re, (row_at, col_at)
    )
    pgrad_re = pgrad_re + piece_re * chi_re + piece_im * chi_im
    pgrad_im = pgrad_im + piece_re * chi_im - piece_im * chi_re
    return (grad_re, grad_im, pgrad_re, pgrad_im)


def per_device(obj_re, obj_im, probe_re, probe_im, amplitude, offsets, counts):
    tile_rows = obj_re.shape[0]
    patch_size = probe_re.shape[0]
    slot_total = amplitude.shape[2]
    tile_x = lax.axis_index("tx")
    side_index = lax.axis_index("ty")
    wide_re, wide_im = (
        lax.all_gather(obj_re, "ty", axis=1, tiled=True),
        lax.all_gather(obj_im, "ty", axis=1, tiled=True),
    )
    col_shift = side_index * 0
    below_re, below_im = passed_along((wide_re, wide_im), "tx", -1)
    region_re = jnp.concatenate([wide_re, below_re], axis=0)
    region_im = jnp.concatenate([wide_im, below_im], axis=0)
    cosine, sine_table = make_tables(patch_size)
    own_amp = amplitude[0, 0]
    places = offsets[0]
    local_rows = places[:, :, 0] - tile_x * tile_rows
    local_cols = places[:, :, 1]
    tile_counts = counts[0]
    start_totals = (
        jnp.zeros_like(region_re),
        jnp.zeros_like(region_im),
        jnp.zeros_like(probe_re),
        jnp.zeros_like(probe_im),
    )

    def own_step(index, totals):
        measured = lax.dynamic_index_in_dim(own_amp, index, 0, keepdims=False)
        row_at = local_rows[side_index, index]
        col_at = local_cols[side_index, index]
        return one_position(
            totals,
            region_re,
            region_im,
            probe_re,
            probe_im,
            cosine,
            sine_table,
            measured,
            row_at,
            col_at,
        )

    totals = lax.fori_loop(0, tile_counts[side_index], own_step, start_totals)
    grad_re, grad_im, pgrad_re, pgrad_im = totals
    owned_re, owned_im = (
        lax.psum_scatter(grad_re, "ty", scatter_dimension=1, tiled=True),
        lax.psum_scatter(grad_im, "ty", scatter_dimension=1, tiled=True),
    )
    top_re = owned_re[:tile_rows]
    top_im = owned_im[:tile_rows]
    came_re, came_im = passed_along((owned_re[tile_rows:], owned_im[tile_rows:]), "tx", 1)
    result_re = top_re + came_re
    result_im = top_im + came_im
    summed_re, summed_im = lax.psum((pgrad_re, pgrad_im), ("tx", "ty"))
    scale_by = 1.0 / (lax.axis_size("tx") * lax.axis_size("ty") * slot_total)
    return (result_re, result_im, summed_re * scale_by, summed_im * scale_by)


def solution(mesh):
    return jax.shard_map(
        per_device,
        mesh=mesh,
        in_specs=(
            P("tx", "ty"),
            P("tx", "ty"),
            P(),
            P(),
            P("tx", "ty", None, None, None),
            P("tx", None, None, None),
            P("tx", None),
        ),
        out_specs=(P("tx", "ty"), P("tx", "ty"), P(), P()),
        check_vma=False,
    )
```

profile of v0, /device:TPU:1, one launch (start us, length us, event | category | flops | bytes accessed | tf_op | source)
XLA Modules:
  0.0 956.4 jit_solution(17858026093120556610)
XLA Ops:
  8.7 32.8 %all-gather.5.cloned.1.call-done = f32[512,512]{1,0:T(8,128)} async-done(((f32[512,256]{1,0:T(8,128)}), f32[512,512]{1,0:T(8,128)}) %all-gather.5.cloned.1.call-update) | async-done | bytes 1048592 | tf_op jit(solution)/shard_map/all_gather | solution.py:69
  41.5 2.6 collective-permute-start.1
  44.1 26.6 %all-gather.3.cloned.1.call-done = f32[512,512]{1,0:T(8,128)} async-done(((f32[512,256]{1,0:T(8,128)}), f32[512,512]{1,0:T(8,128)}) %all-gather.3.cloned.1.call-update) | async-done | bytes 1048592 | tf_op jit(solution)/shard_map/all_gather | solution.py:68
  70.7 2.6 collective-permute-start
  74.7 2.9 pad_maximum_fusion.1
  77.6 9.5 collective-permute-done
  89.6 1.6 broadcast.25
  91.2 217.9 %while.20 = (s32[]{:T(128)}, f32[1024,512]{1,0:T(8,128)}, f32[1024,512]{1,0:T(8,128)S(1)}, f32[256,256]{1,0:T(8,128)}, f32[256,256]{1,0:T(8,128)S(1)}, /*index=5...) while((s32[]{:T(128)}, f32[1024,512]{1,0:T(8,128)}, ...), condition=%wide.region_1.2_spmd.clone.clone, body=%wide.region_0.1_spmd.clone.clone.sunk | while | flops 3239444480 | bytes 19136904 | solution.py:105
  100.0 1.5 convolution_subtract_fusion.7
  107.4 1.5 convolution_subtract_fusion.8
  108.9 2.5 fusion.163
  120.4 1.5 convolution_add_fusion.9
  121.9 3.0 multiply_subtract_fusion.6
  125.6 3.9 dynamic_update_slice.16
  129.5 5.3 dynamic_update_slice.17
  151.1 1.5 convolution_subtract_fusion.8
  152.6 2.5 fusion.163
  164.0 1.5 convolution_add_fusion.9
  165.5 3.0 multiply_subtract_fusion.6
  169.3 3.9 dynamic_update_slice.16
  173.1 5.3 dynamic_update_slice.17
  194.7 1.5 convolution_subtract_fusion.8
  196.2 2.5 fusion.163
  207.6 1.5 convolution_add_fusion.9
  209.1 3.0 multiply_subtract_fusion.6
  212.9 3.6 dynamic_update_slice.16
  216.5 4.7 dynamic_update_slice.17
  237.4 1.5 convolution_subtract_fusion.8
  238.9 2.5 fusion.163
  250.3 1.5 convolution_add_fusion.9
  251.8 3.0 multiply_subtract_fusion.6
  255.5 3.9 dynamic_update_slice.16
  259.4 5.3 dynamic_update_slice.17
  273.6 1.5 convolution_subtract_fusion.7
  281.0 1.5 convolution_subtract_fusion.8
  282.5 2.5 fusion.163
  294.0 1.5 convolution_add_fusion.9
  295.5 3.0 multiply_subtract_fusion.6
  299.2 3.9 dynamic_update_slice.16
  303.1 5.3 dynamic_update_slice.17
  310.5 339.0 %reduce-scatter.3.cloned.1.call-done = f32[1024,256]{1,0:T(8,128)} async-done(((f32[1024,512]{1,0:T(8,128)}), f32[1024,256]{1,0:T(8,128)}) %reduce-scatter.3.cloned.1.call-update) | async-done | bytes 1048592 | tf_op jit(solution)/shard_map/reduce_scatter | solution.py:108
  649.5 2.0 slice.27
  651.4 3.7 collective-permute-start.2
  655.1 34.8 %reduce-scatter.5.cloned.1.call-done = f32[1024,256]{1,0:T(8,128)} async-done(((f32[1024,512]{1,0:T(8,128)}), f32[1024,256]{1,0:T(8,128)}) %reduce-scatter.5.cloned.1.call-update) | async-done | bytes 1048592 | tf_op jit(solution)/shard_map/reduce_scatter | solution.py:109
  689.9 2.0 slice.29
  691.8 3.7 collective-permute-start.3
  695.5 250.8 %all-reduce.3.cloned.1.call-done = (f32[256,256]{1,0:T(8,128)}, f32[256,256]{1,0:T(8,128)}) async-done(((f32[256,256]{1,0:T(8,128)}, f32[256,256]{1,0:T(8,128)}), (f32[256,256]{1,0:T(8,128)}, f32[256,256]{1,0:T(8,128)})) %all-reduce.3.cloned.1.call-update) | async-done | bytes 524304 | tf_op jit(solution)/shard_map/psum | solution.py:116
  946.3 1.9 broadcast_multiply_fusion
  (130 shorter events, 110.6 us)
Async XLA Ops:
  7.2 66.2 %copy-start = (s32[1,2]{1,0:T(1,128)S(1)}, s32[1,2]{1,0:T(1,128)}, u32[]{:S(2)}) copy-start(s32[1,2]{1,0:T(1,128)} %param.15) | copy-start | bytes 28
  7.2 34.4 %all-gather.5.cloned.1.call-start = ((), (), s32[]{:S(2)}) async-start(), calls=%async_computation.3 | async-start | bytes 1572864 | tf_op jit(solution)/shard_map/all_gather | solution.py:69
  7.9 62.8 %all-gather.3.cloned.1.call-start = ((), (), s32[]{:S(2)}) async-start(), calls=%async_computation.2 | async-start | bytes 1572864 | tf_op jit(solution)/shard_map/all_gather | solution.py:68
  8.7 640.8 %reduce-scatter.3.cloned.1.call-start = ((), (), s32[]{:S(2)}) async-start(), calls=%async_computation.4 | async-start | bytes 3145728 | tf_op jit(solution)/shard_map/reduce_scatter | solution.py:108
  41.5 33.1 %collective-permute-start.1 = (f32[512,512]{1,0:T(8,128)}, f32[512,512]{1,0:T(8,128)S(1)}, u32[]{:S(2)}, u32[]{:S(2)}) collective-permute-start(f32[512,512]{1,0:T(8,128)} %all-gather.5.cloned.1.call-done), channel_id=1, source_target_pairs={{2,0},{4,2},{6,4},{8,6},{10,8},{12,10},{14,12},{16,14},{18,16},{20... | collective-permute-start | bytes 3145736 | tf_op jit(solution)/shard_map/ppermute | solution.py:12
  70.7 16.3 %collective-permute-start = (f32[512,512]{1,0:T(8,128)}, f32[512,512]{1,0:T(8,128)S(1)}, u32[]{:S(2)}, u32[]{:S(2)}) collective-permute-start(f32[512,512]{1,0:T(8,128)} %all-gather.3.cloned.1.call-done), channel_id=1, source_target_pairs={{2,0},{4,2},{6,4},{8,6},{10,8},{12,10},{14,12},{16,14},{18,16},{20... | collective-permute-start | bytes 3145736 | tf_op jit(solution)/shard_map/ppermute | solution.py:12
  74.7 12.4 %copy-start.9 = (f32[512,512]{1,0:T(8,128)S(1)}, f32[512,512]{1,0:T(8,128)}, u32[]{:S(2)}) copy-start(f32[512,512]{1,0:T(8,128)} %all-gather.3.cloned.1.call-done) | copy-start | bytes 3145732
  89.3 1.9 copy-start.1
  89.3 1.9 copy-start.2
  117.4 4.5 copy-start.5
  124.9 0.7 copy-start.6
  161.1 4.5 copy-start.5
  168.6 0.7 copy-start.6
  204.7 4.5 copy-start.5
  212.2 0.7 copy-start.6
  247.3 4.5 copy-start.5
  254.8 0.7 copy-start.6
  291.0 4.5 copy-start.5
  298.5 0.7 copy-start.6
  309.1 1.3 copy-start.3
  309.1 1.4 copy-start.4
  309.1 380.7 %reduce-scatter.5.cloned.1.call-start = ((), (), s32[]{:S(2)}) async-start(), calls=%async_computation.5 | async-start | bytes 3145728 | tf_op jit(solution)/shard_map/reduce_scatter | solution.py:109
  310.5 635.8 %all-reduce.3.cloned.1.call-start = ((), (), s32[]{:S(2)}) async-start(), calls=%async_computation.6 | async-start | bytes 1048576 | tf_op jit(solution)/shard_map/psum | solution.py:116
  649.5 298.7 %copy-start.7 = (f32[1024,256]{1,0:T(8,128)S(1)}, f32[1024,256]{1,0:T(8,128)}, u32[]{:S(2)}) copy-start(f32[1024,256]{1,0:T(8,128)} %reduce-scatter.3.cloned.1.call-done) | copy-start | bytes 3145732
  651.4 296.8 %collective-permute-start.2 = (f32[512,256]{1,0:T(8,128)}, f32[512,256]{1,0:T(8,128)S(1)}, u32[]{:S(2)}, u32[]{:S(2)}) collective-permute-start(f32[512,256]{1,0:T(8,128)} %slice.27), channel_id=1, source_target_pairs={{0,2},{2,4},{4,6},{6,8},{8,10},{10,12},{12,14},{14,16},{16,18},{18... | collective-permute-start | bytes 1572872 | tf_op jit(solution)/shard_map/ppermute | solution.py:12
  689.9 259.2 %copy-start.8 = (f32[1024,256]{1,0:T(8,128)S(1)}, f32[1024,256]{1,0:T(8,128)}, u32[]{:S(2)}) copy-start(f32[1024,256]{1,0:T(8,128)} %reduce-scatter.5.cloned.1.call-done) | copy-start | bytes 3145732
  691.8 257.2 %collective-permute-start.3 = (f32[512,256]{1,0:T(8,128)}, f32[512,256]{1,0:T(8,128)S(1)}, u32[]{:S(2)}, u32[]{:S(2)}) collective-permute-start(f32[512,256]{1,0:T(8,128)} %slice.29), channel_id=1, source_target_pairs={{0,2},{2,4},{4,6},{6,8},{8,10},{10,12},{12,14},{14,16},{16,18},{18... | collective-permute-start | bytes 1572872 | tf_op jit(solution)/shard_map/ppermute | solution.py:12
Sparse Core Ops, SparseCore 0:
  9.8 31.6 all-gather.4
  43.3 27.3 all-gather.2
  309.2 340.1 reduce-scatter.2
  652.0 37.8 reduce-scatter.4
  695.9 250.3 all-reduce.2
where the time goes:
time: 960 us; the launch traced here: 956 us
  waiting for transfers between devices  695 us (72%)
  matrix products  131 us (14%)
  local copies, waits for them, and re-layouts  63.6 us (7%)
  loops' own time  25 us (3%)
  other arithmetic  15.5 us (2%)
  between operations  13.9 us (1%)
  starting transfers between devices  12.6 us (1%)
    reduce_scatter x1, waiting for transfers between devices, per_device(): lax.psum_scatter(grad_re, 'ty', scatter_dimension=1, tiled=True)  339 us
    psum x1, waiting for transfers between devices, per_device(): summed_re, summed_im = lax.psum((pgrad_re, pgrad_im), ('tx', 'ty'))  251 us
    dot_general x80, matrix products, matmul(): jnp.dot(left, right, precision=lax.Precision.HIGHEST, preferred_element_t...  131 us
    reduce_scatter x1, waiting for transfers between devices, per_device(): lax.psum_scatter(grad_im, 'ty', scatter_dimension=1, tiled=True)  34.8 us
    all_gather x1, waiting for transfers between devices, per_device(): lax.all_gather(obj_im, 'ty', axis=1, tiled=True)  32.8 us
    all_gather x1, waiting for transfers between devices, per_device(): lax.all_gather(obj_re, 'ty', axis=1, tiled=True)  26.6 us
    dynamic_update_slice x5, local copies, waits for them, and re-layouts, one_position(): lax.dynamic_update_slice(grad_im, now_im + probe_re * chi_im - probe_im *...  25.9 us
    another operation x1, loops' own time, per_device(): totals = lax.fori_loop(0, tile_counts[side_index], own_step, start_totals)  25 us
  transfers between devices with their start and end apart: 9, of which 6 were waited for; matrix products, arithmetic and copies ran while one was open for 1% of the time, Pallas kernels for 0%

commit v1 on v0

v1 whole, which is shorter than its diff:
```python
import math

import jax
import jax.numpy as jnp
import ml_dtypes
import numpy as np
from jax import lax
from jax.experimental import pallas as pl
from jax.experimental.pallas import tpu as pltpu
from jax.sharding import PartitionSpec as P

N = 256
H = 128
TR = 512
SLOTS = 12
NTX = 128
ROWS = TR + N
MESH = pl.DeviceIdType.MESH
F32 = jnp.float32
BF16 = jnp.bfloat16


def half_dft_tables():
    n = np.arange(H, dtype=np.float64)[:, None]
    k = np.arange(H, dtype=np.float64)[None, :]
    tables = []
    for odd in (0, 1):
        angle = -2.0 * math.pi * (n * (2 * k + odd)) / N
        re, im = np.cos(angle) / 16.0, np.sin(angle) / 16.0
        tables.append(np.block([[re, im], [-im, re]]))
    both = np.stack([tables[0], tables[1], tables[0].T, tables[1].T])
    high = both.astype(ml_dtypes.bfloat16)
    low = (both - high.astype(np.float64)).astype(ml_dtypes.bfloat16)
    return np.stack([high, low])


def even_odd_lanes():
    table = np.zeros((N, N), np.float32)
    j = np.arange(H)
    table[2 * j, j] = 1.0
    table[2 * j + 1, H + j] = 1.0
    return table.astype(ml_dtypes.bfloat16)


def split(x):
    high = x.astype(BF16)
    return high, (x - high.astype(F32)).astype(BF16)


def dot(a, b):
    return jnp.dot(a, b, preferred_element_type=F32)


def halo_kernel(
    obj_re, obj_im, amp, perm, reg, amp_out, raw, sorted_amp,
    ty_send, ty_recv, up_send, up_recv, diag_send, diag_recv, own_sem, raw_sem, amp_sem,
):
    tx, ty = lax.axis_index("tx"), lax.axis_index("ty")
    up, down = lax.rem(tx + NTX - 1, NTX), lax.rem(tx + 1, NTX)
    partner = (tx, 1 - ty)
    barrier = pltpu.get_barrier_semaphore()
    for device in (partner, (up, ty), (down, ty)):
        pl.semaphore_signal(barrier, inc=1, device_id=device, device_id_type=MESH)
    raw_copies = []
    for t in range(2):
        c = pltpu.make_async_copy(amp.at[0, 0, :, :, pl.ds(t * H, H)], raw.at[t], raw_sem.at[t])
        c.start()
        raw_copies.append(c)
    own = []
    for p, obj in enumerate((obj_re, obj_im)):
        for t in range(2):
            c = pltpu.make_async_copy(
                obj.at[:, pl.ds(t * H, H)], reg.at[p, ty + t, pl.ds(0, TR)], own_sem.at[p, t])
            c.start()
            own.append(c)
    pl.semaphore_wait(barrier, 3)

    edge = pl.multiple_of((1 - ty) * H, H)
    across = [[], []]
    for half in range(2):
        for p, obj in enumerate((obj_re, obj_im)):
            rows = pl.ds(half * N, N)
            c = pltpu.make_async_remote_copy(
                src_ref=obj.at[rows, pl.ds(edge, H)], dst_ref=reg.at[p, 2 * ty, rows],
                send_sem=ty_send.at[half, p], recv_sem=ty_recv.at[half, p],
                device_id=partner, device_id_type=MESH)
            c.start()
            across[half].append(c)
    below = []
    for p, obj in enumerate((obj_re, obj_im)):
        for t in range(2):
            c = pltpu.make_async_remote_copy(
                src_ref=obj.at[pl.ds(0, N), pl.ds(t * H, H)], dst_ref=reg.at[p, ty + t, pl.ds(TR, N)],
                send_sem=up_send.at[p, t], recv_sem=up_recv.at[p, t],
                device_id=(up, ty), device_id_type=MESH)
            c.start()
            below.append(c)
    for c in raw_copies:
        c.wait()

    def sort_slot(i, carry):
        for h in range(2):
            rows = [raw[t, i, pl.ds(h, H, stride=2), :] for t in range(2)]
            high, low = split(jnp.concatenate(rows, axis=1))
            sorted_amp[i, pl.ds(h * H, H), :] = dot(high, perm[...]) + dot(low, perm[...])
        pltpu.make_async_copy(sorted_amp.at[i], amp_out.at[i], amp_sem.at[i]).start()
        return carry

    lax.fori_loop(0, SLOTS // 2, sort_slot, 0)
    diag = []
    for p in range(2):
        across[0][p].wait()
        side = 2 - 2 * ty
        c = pltpu.make_async_remote_copy(
            src_ref=reg.at[p, side, pl.ds(0, N)], dst_ref=reg.at[p, side, pl.ds(TR, N)],
            send_sem=diag_send.at[p], recv_sem=diag_recv.at[p],
            device_id=(up, ty), device_id_type=MESH)
        c.start()
        diag.append(c)
    lax.fori_loop(SLOTS // 2, SLOTS, sort_slot, 0)

    def finish_slot(i, carry):
        pltpu.make_async_copy(sorted_amp.at[i], amp_out.at[i], amp_sem.at[i]).wait()
        return carry

    lax.fori_loop(0, SLOTS, finish_slot, 0)
    for c in own + across[1] + below + diag:
        c.wait()


def halo(obj_re, obj_im, amp, perm):
    anywhere = pl.BlockSpec(memory_space=pl.ANY)
    dma = pltpu.SemaphoreType.DMA
    return pl.pallas_call(
        halo_kernel,
        out_shape=(
            jax.ShapeDtypeStruct((2, 3, ROWS, H), F32),
            jax.ShapeDtypeStruct((SLOTS, N, N), F32),
        ),
        in_specs=[anywhere, anywhere, anywhere, pl.BlockSpec(memory_space=pltpu.VMEM)],
        out_specs=(anywhere, anywhere),
        scratch_shapes=[
            pltpu.VMEM((2, SLOTS, N, H), F32),
            pltpu.VMEM((SLOTS, N, N), F32),
            dma((2, 2)), dma((2, 2)), dma((2, 2)), dma((2, 2)), dma((2,)), dma((2,)),
            dma((2, 2)), dma((2,)), dma((SLOTS,)),
        ],
        compiler_params=pltpu.CompilerParams(
            collective_id=0, has_side_effects=True, vmem_limit_bytes=40 << 20),
        name="halo",
    )(obj_re, obj_im, amp, perm)


def positions_kernel(
    offsets, counts, reg, probe_re, probe_im, tables, amp_in, grad, pgrad,
    amp, win, sp, mid, amp_sem,
):
    tx, ty = lax.axis_index("tx"), lax.axis_index("ty")
    live = counts[0, ty]
    probe = (probe_re, probe_im)
    CH = 32

    def fetch(i):
        return pltpu.make_async_copy(amp_in.at[i], amp.at[i], amp_sem.at[i])

    def start_fetch(i, carry):
        fetch(i).start()
        return carry

    lax.fori_loop(0, live, start_fetch, 0)
    grad[...] = jnp.zeros_like(grad)
    pgrad[...] = jnp.zeros_like(pgrad)
    lane = lax.broadcasted_iota(jnp.int32, (CH, H), 1)

    def put(q, rows, lanes, value):
        high, low = split(value)
        sp[0, q, rows, lanes] = high
        sp[1, q, rows, lanes] = low

    def right(q, which):
        return (dot(sp[0, q], tables[0, which]) + dot(sp[1, q], tables[0, which])
                + dot(sp[0, q], tables[1, which]))

    def left(q, which):
        return (dot(tables[0, which], sp[0, q]) + dot(tables[1, which], sp[0, q])
                + dot(tables[0, which], sp[1, q]))

    def lanes(t):
        return pl.ds(t * H, H)

    def one(i, carry):
        row_at = offsets[0, ty, i, 0] - tx * TR
        col_at = offsets[0, ty, i, 1] - ty * H
        back = lax.rem(H - col_at, H)
        ahead = lax.rem(col_at, H)
        from_next = lane >= H - col_at
        to_next = lane < col_at
        for j in range(N // CH):
            rows = pl.ds(j * CH, CH)
            ex = [[None, None], [None, None]]
            w = [[None, None], [None, None]]
            for p in range(2):
                turned = [pltpu.roll(reg[p, t, pl.ds(row_at + j * CH, CH), :], back, 1) for t in range(3)]
                for t in range(2):
                    w[p][t] = jnp.where(from_next, turned[t + 1], turned[t])
                    win[p, t, rows, :] = w[p][t]
            for t in range(2):
                pr, pi = probe_re[rows, lanes(t)], probe_im[rows, lanes(t)]
                ex[0][t] = pr * w[0][t] - pi * w[1][t]
                ex[1][t] = pr * w[1][t] + pi * w[0][t]
            for p in range(2):
                put(0, rows, lanes(p), ex[p][0] + ex[p][1])
                put(1, rows, lanes(p), ex[p][0] - ex[p][1])
        for q in range(2):
            mid[q] = right(q, q)
        for j in range(H // CH):
            for q in range(2):
                for p in range(2):
                    top = mid[q, pl.ds(j * CH, CH), lanes(p)]
                    low = mid[q, pl.ds(H + j * CH, CH), lanes(p)]
                    rows = pl.ds(p * H + j * CH, CH)
                    put(0, rows, lanes(q), top + low)
                    put(1, rows, lanes(q), top - low)
        for h in range(2):
            mid[h] = left(h, 2 + h)
        fetch(i).wait()
        for j in range(H // CH):
            for h in range(2):
                rows_re, rows_im = pl.ds(j * CH, CH), pl.ds(H + j * CH, CH)
                re, im = mid[h, rows_re, :], mid[h, rows_im, :]
                measured = amp[i, pl.ds(h * H + j * CH, CH), :]
                keep = 1.0 - measured * lax.rsqrt(jnp.maximum(re * re + im * im, 1.0))
                put(h, rows_re, slice(None), re * keep)
                put(h, rows_im, slice(None), im * keep)
        for h in range(2):
            mid[h] = left(h, h)
        for j in range(H // CH):
            for p in range(2):
                for q in range(2):
                    a = mid[0, pl.ds(p * H + j * CH, CH), lanes(q)]
                    b = mid[1, pl.ds(p * H + j * CH, CH), lanes(q)]
                    put(q, pl.ds(j * CH, CH), lanes(p), a + b)
                    put(q, pl.ds(H + j * CH, CH), lanes(p), a - b)
        for q in range(2):
            mid[q] = right(q, 2 + q)
        for j in range(N // CH):
            rows = pl.ds(j * CH, CH)
            g = [[None, None], [None, None]]
            for t in range(2):
                chi = []
                for p in range(2):
                    a, b = mid[0, rows, lanes(p)], mid[1, rows, lanes(p)]
                    chi.append(a + b if t == 0 else a - b)
                pr, pi = probe_re[rows, lanes(t)], probe_im[rows, lanes(t)]
                wr, wi = win[0, t, rows, :], win[1, t, rows, :]
                g[0][t] = pltpu.roll(pr * chi[0] + pi * chi[1], ahead, 1)
                g[1][t] = pltpu.roll(pr * chi[1] - pi * chi[0], ahead, 1)
                pgrad[0, t, rows, :] += wr * chi[0] + wi * chi[1]
                pgrad[1, t, rows, :] += wr * chi[1] - wi * chi[0]
            at = pl.ds(row_at + j * CH, CH)
            for p in range(2):
                grad[p, 0, at, :] += jnp.where(to_next, 0.0, g[p][0])
                grad[p, 1, at, :] += jnp.where(to_next, g[p][0], g[p][1])
                grad[p, 2, at, :] += jnp.where(to_next, g[p][1], 0.0)
        return carry

    lax.fori_loop(0, live, one, 0)


def positions(offsets, counts, reg, probe_re, probe_im, tables, amp):
    smem = pl.BlockSpec(memory_space=pltpu.SMEM)
    vmem = pl.BlockSpec(memory_space=pltpu.VMEM)
    return pl.pallas_call(
        positions_kernel,
        out_shape=(
            jax.ShapeDtypeStruct((2, 3, ROWS, H), F32),
            jax.ShapeDtypeStruct((2, 2, N, H), F32),
        ),
        in_specs=[smem, smem, vmem, vmem, vmem, vmem, pl.BlockSpec(memory_space=pl.ANY)],
        out_specs=(vmem, vmem),
        scratch_shapes=[
            pltpu.VMEM((SLOTS, N, N), F32),
            pltpu.VMEM((2, 2, N, H), F32),
            pltpu.VMEM((2, 2, N, N), BF16),
            pltpu.VMEM((2, N, N), F32),
            pltpu.SemaphoreType.DMA((SLOTS,)),
        ],
        compiler_params=pltpu.CompilerParams(vmem_limit_bytes=40 << 20),
        name="positions",
    )(offsets, counts, reg, probe_re, probe_im, tables, amp)


def out_kernel(
    grad, pgrad, out_re, out_im, pout_re, pout_im,
    came_ty, came_up, came_diag, edge, core_in, acc, y_in, z_in, x_all, full, other,
    ty_send, ty_recv, up_send, up_recv, diag_send, diag_recv,
    core_send, core_recv, y_send, y_recv, z_send, z_recv, x_send, x_recv,
):
    tx, ty = lax.axis_index("tx"), lax.axis_index("ty")
    up, down = lax.rem(tx + NTX - 1, NTX), lax.rem(tx + 1, NTX)
    partner = (tx, 1 - ty)
    core, y, z, x_lo = lax.rem(tx, 2), lax.rem(tx // 2, 4), lax.rem(tx // 8, 8), tx // 64
    x = ty * 2 + x_lo

    def at(core_, y_, z_, x_):
        return (((lax.rem(x_, 2) * 8 + z_) * 4 + y_) * 2 + core_, x_ // 2)

    core_mate = at(1 - core, y, z, x)
    y_mates = [at(core, lax.rem(y + d, 4), z, x) for d in range(1, 4)]
    z_mates = [at(core, y, lax.rem(z + d, 8), x) for d in range(1, 8)]
    x_mates = [at(core, y, z, lax.rem(x + d, 4)) for d in range(1, 4)]
    greeted = [partner, (up, ty), (down, ty), core_mate] + y_mates + z_mates + x_mates
    barrier = pltpu.get_barrier_semaphore()
    for device in greeted:
        pl.semaphore_signal(barrier, inc=1, device_id=device, device_id_type=MESH)
    pl.semaphore_wait(barrier, len(greeted))

    def send(src, dst, send_sem, recv_sem, device):
        c = pltpu.make_async_remote_copy(
            src_ref=src, dst_ref=dst, send_sem=send_sem, recv_sem=recv_sem,
            device_id=device, device_id_type=MESH)
        c.start()
        return c

    side = 2 - 2 * ty
    core_copy = send(pgrad.at[1 - core], core_in, core_send.at[0], core_recv.at[0], core_mate)
    diag = send(grad.at[:, side, pl.ds(TR, N)], came_diag, diag_send, diag_recv, (down, ty))
    far_rows = send(
        grad.at[:, side, pl.ds(N, N)], came_ty.at[:, pl.ds(N, N)], ty_send.at[1], ty_recv.at[1], partner)
    below = send(
        grad.at[:, pl.ds(ty, 2), pl.ds(TR, N)], came_up, up_send, up_recv, (down, ty))

    core_copy.wait()
    for t in range(2):
        acc[pl.ds(t * N, N), :] = pgrad[core, t] + core_in[t]
    y_copies = [
        send(acc.at[pl.ds(pl.multiple_of(lax.rem(y + d, 4) * H, H), H)], y_in.at[d - 1],
             y_send.at[0, d - 1], y_recv.at[0, d - 1], y_mates[d - 1])
        for d in range(1, 4)]

    diag.wait()
    for p in range(2):
        edge[p] = grad[p, side, pl.ds(0, N)] + came_diag[p]
    near_rows = send(edge, came_ty.at[:, pl.ds(0, N)], ty_send.at[0], ty_recv.at[0], partner)

    for c in y_copies:
        c.wait()
    y_rows = pl.ds(pl.multiple_of(y * H, H), H)
    acc[y_rows, :] = acc[y_rows, :] + y_in[0] + y_in[1] + y_in[2]
    z_copies = [
        send(acc.at[pl.ds(pl.multiple_of(y * H + lax.rem(z + d, 8) * 16, 16), 16)], z_in.at[d - 1],
             z_send.at[0, d - 1], z_recv.at[0, d - 1], z_mates[d - 1])
        for d in range(1, 8)]
    for c in z_copies:
        c.wait()
    z_rows = pl.ds(pl.multiple_of(y * H + z * 16, 16), 16)
    total = acc[z_rows, :]
    for d in range(7):
        total = total + z_in[d]
    x_all[x] = total
    x_copies = [
        send(x_all.at[x], x_all.at[x], x_send.at[d - 1], x_recv.at[d - 1], x_mates[d - 1])
        for d in range(1, 4)]
    for c in x_copies:
        c.wait()
    full[z_rows, :] = ((x_all[0] + x_all[1]) + (x_all[2] + x_all[3])) * (1.0 / (NTX * 2 * SLOTS))
    z_copies = [
        send(full.at[z_rows], full.at[z_rows], z_send.at[1, d - 1], z_recv.at[1, d - 1], z_mates[d - 1])
        for d in range(1, 8)]
    for c in z_copies:
        c.wait()
    y_copies = [
        send(full.at[y_rows], full.at[y_rows], y_send.at[1, d - 1], y_recv.at[1, d - 1], y_mates[d - 1])
        for d in range(1, 4)]
    for c in y_copies:
        c.wait()
    core_copy = send(full, other, core_send.at[1], core_recv.at[1], core_mate)

    below.wait()
    far_rows.wait()
    near_rows.wait()
    for p, out in enumerate((out_re, out_im)):
        for t in range(2):
            lanes = pl.ds(t * H, H)
            mine = ty == 1 - t
            ty_rows = [jnp.where(mine, came_ty[p, pl.ds(h * N, N)], 0.0) for h in range(2)]
            out[pl.ds(0, N), lanes] = (
                grad[p, ty + t, pl.ds(0, N)] + came_up[p, t] + ty_rows[0])
            out[pl.ds(N, N), lanes] = grad[p, ty + t, pl.ds(N, N)] + ty_rows[1]
    core_copy.wait()
    for t in range(2):
        rows, lanes = pl.ds(t * N, N), pl.ds(t * H, H)
        a, b = full[rows, :], other[rows, :]
        pout_re[:, lanes] = jnp.where(core == 0, a, b)
        pout_im[:, lanes] = jnp.where(core == 0, b, a)


def gather_out(grad, pgrad):
    vmem = pl.BlockSpec(memory_space=pltpu.VMEM)
    dma = pltpu.SemaphoreType.DMA
    tile = jax.ShapeDtypeStruct((TR, N), F32)
    patch = jax.ShapeDtypeStruct((N, N), F32)
    return pl.pallas_call(
        out_kernel,
        out_shape=(tile, tile, patch, patch),
        in_specs=[vmem, vmem],
        out_specs=(vmem, vmem, vmem, vmem),
        scratch_shapes=[
            pltpu.VMEM((2, TR, H), F32),
            pltpu.VMEM((2, 2, N, H), F32),
            pltpu.VMEM((2, N, H), F32),
            pltpu.VMEM((2, N, H), F32),
            pltpu.VMEM((2, N, H), F32),
            pltpu.VMEM((2 * N, H), F32),
            pltpu.VMEM((3, H, H), F32),
            pltpu.VMEM((7, 16, H), F32),
            pltpu.VMEM((4, 16, H), F32),
            pltpu.VMEM((2 * N, H), F32),
            pltpu.VMEM((2 * N, H), F32),
            dma((2,)), dma((2,)), dma(()), dma(()), dma(()), dma(()),
            dma((2,)), dma((2,)), dma((2, 3)), dma((2, 3)), dma((2, 7)), dma((2, 7)), dma((3,)), dma((3,)),
        ],
        compiler_params=pltpu.CompilerParams(
            collective_id=1, has_side_effects=True, vmem_limit_bytes=40 << 20),
        name="gather_out",
    )(grad, pgrad)


def per_device(obj_re, obj_im, probe_re, probe_im, amplitude, offsets, counts):
    tables = jnp.asarray(half_dft_tables())
    perm = jnp.asarray(even_odd_lanes())
    reg, amp = halo(obj_re, obj_im, amplitude, perm)
    grad, pgrad = positions(offsets, counts, reg, probe_re, probe_im, tables, amp)
    return gather_out(grad, pgrad)


def solution(mesh):
    return jax.shard_map(
        per_device,
        mesh=mesh,
        in_specs=(
            P("tx", "ty"),
            P("tx", "ty"),
            P(),
            P(),
            P("tx", "ty", None, None, None),
            P("tx", None, None, None),
            P("tx", None),
        ),
        out_specs=(P("tx", "ty"), P("tx", "ty"), P(), P()),
        check_vma=False,
    )
```

time: 960 us -> 96.8 us (0.10)
  waiting for transfers between devices: 695 us -> 0 us
  matrix products: 131 us -> 0 us
  Pallas kernels: 0 us -> 87.1 us
  local copies, waits for them, and re-layouts: 63.6 us -> 8.66 us
  loops' own time: 25 us -> 0 us
  other arithmetic: 15.5 us -> 0 us
  between operations: 13.9 us -> 0.7 us
  starting transfers between devices: 12.6 us -> 0 us
    reduce_scatter x2 -> x0, waiting for transfers between devices: 374 us -> none  [the longest x1 339 us: per_device(): lax.psum_scatter(grad_re, 'ty', scatter_dimension=1, tiled=True)]
    psum x1 -> x0, waiting for transfers between devices: 251 us -> none  [per_device(): summed_re, summed_im = lax.psum((pgrad_re, pgrad_im), ('tx', 'ty'))]
    dot_general x80 -> x0, matrix products: 131 us -> none  [matmul(): jnp.dot(left, right, precision=lax.Precision.HIGHEST, preferred_element_t...]
    pallas_call x0 -> x3, Pallas kernels: none -> 87.1 us  [the longest x1 61.4 us: gather_out(): pl.pallas_call(out_kernel, out_shape=(tile, tile, patch, patch), in_specs...]
    all_gather x2 -> x0, waiting for transfers between devices: 59.4 us -> none  [the longest x1 32.8 us: per_device(): lax.all_gather(obj_im, 'ty', axis=1, tiled=True)]
    dynamic_update_slice x10 -> x0, local copies, waits for them, and re-layouts: 45.1 us -> none  [the longest x5 25.9 us: one_position(): lax.dynamic_update_slice(grad_im, now_im + probe_re * chi_im - probe_im *...]
    another operation x1 -> x0, loops' own time: 25 us -> none  [per_device(): totals = lax.fori_loop(0, tile_counts[side_index], own_step, start_totals)]
    ppermute x4 -> x0, starting transfers between devices: 12.4 us -> none  [passed_along(): lax.ppermute(value, axis, [(source, source + steps) for source in range(i...]
  transfers between devices with their start and end apart: 9 -> 0, of which waited for: 6 -> 0; matrix products, arithmetic and copies ran while one was open for 1% -> 0% of each run, Pallas kernels for 0% -> 0%
where the time goes in v1:
time: 96.8 us; the launch traced here: 96.5 us
  Pallas kernels  87.1 us (90%)
  local copies, waits for them, and re-layouts  8.66 us (9%)
    pallas_call x1, Pallas kernels, gather_out(): pl.pallas_call(out_kernel, out_shape=(tile, tile, patch, patch), in_specs...  61.4 us
    pallas_call x1, Pallas kernels, halo(): pl.pallas_call(halo_kernel, out_shape=(jax.ShapeDtypeStruct((2, 3, ROWS,...  16.2 us
    pallas_call x1, Pallas kernels, positions(): pl.pallas_call(positions_kernel, out_shape=(jax.ShapeDtypeStruct((2, 3, R...  9.53 us
    unnamed x21, local copies, waits for them, and re-layouts  8.66 us

profile of v1, /device:TPU:1, one launch (start us, length us, event | category | flops | bytes accessed | tf_op | source)
XLA Modules:
  0.0 96.5 jit_solution(7326811974293950294)
XLA Ops:
  0.6 0.0 copy-start.7
  0.6 0.8 copy.13.offsets
  1.4 0.0 copy-start
  1.4 1.9 %copy-done = f32[1,1,12,256,256]{4,3,2,1,0:T(8,128)S(1)} copy-done((f32[1,1,12,256,256]{4,3,2,1,0:T(8,128)S(1)}, f32[1,1,12,256,256]{4,3,2,1,0:T(8,128)}, u32[]{:S(2)}) %copy-start) | copy-done | bytes 3145752
  3.3 0.0 copy-start.2
  3.3 1.0 %copy-done.2 = f32[512,256]{1,0:T(8,128)S(1)} copy-done((f32[512,256]{1,0:T(8,128)S(1)}, f32[512,256]{1,0:T(8,128)}, u32[]{:S(2)}) %copy-start.2) | copy-done | bytes 524312
  4.4 0.0 copy-start.3
  4.4 1.0 %copy-done.3 = f32[512,256]{1,0:T(8,128)S(1)} copy-done((f32[512,256]{1,0:T(8,128)S(1)}, f32[512,256]{1,0:T(8,128)}, u32[]{:S(2)}) %copy-start.3) | copy-done | bytes 524312
  5.4 0.0 copy-start.6
  5.4 0.9 copy-done.6
  6.3 0.0 copy-start.1
  6.3 0.0 copy-start.4
  6.3 0.0 copy-start.5
  6.3 16.2 %halo.1 = (f32[2,3,768,128]{3,2,1,0:T(8,128)S(1)}, f32[12,256,256]{2,1,0:T(8,128)S(1)}) custom-call(f32[512,256]{1,0:T(8,128)S(1)} %copy-done.2, f32[512,256]{1,0:T(8,128)S(1)} %copy-done.3, f32[1,1,12,256,256]{4,3,2,1,0:T(8,128)S(1)} %copy-done, bf16[256,256]{1,0:T(8,128)(2,1)S(1)} %copy-done.6), custom_call_target="tpu_custom_call" | custom-call | tf_op jit(solution)/shard_map/halo/pallas_call | solution.py:134
  22.5 0.0 copy-done.7
  22.5 0.0 copy-done.1
  22.6 0.0 copy-done.4
  22.6 0.0 copy-done.5
  22.6 9.5 %positions.1 = (f32[2,3,768,128]{3,2,1,0:T(8,128)S(1)}, f32[2,2,256,128]{3,2,1,0:T(8,128)S(1)}) custom-call(s32[1,2,12,2]{3,2,1,0:T(8,128)S(1)} %copy.13.offsets, s32[1,2]{1,0:T(1,128)S(1)} %copy-done.7, f32[2,3,768,128]{3,2,1,0:T(8,128)S(1)} %get-tuple-element.8.reg, f32[256,256]{1,0:T(8,128)S(1)} %copy-done.4, f32[256,256]{1,0:T(8,128)S(1)} %copy-done.5, ...), custom_call_target="tpu_custom_call" | custom-call | tf_op jit(solution)/shard_map/positions/pallas_call | solution.py:273
  32.1 61.4 %gather_out.1 = (f32[512,256]{1,0:T(8,128)S(1)}, f32[512,256]{1,0:T(8,128)S(1)}, f32[256,256]{1,0:T(8,128)S(1)}, f32[256,256]{1,0:T(8,128)S(1)}) custom-call(f32[2,3,768,128]{3,2,1,0:T(8,128)S(1)} %get-tuple-element.10.grad, f32[2,2,256,128]{3,2,1,0:T(8,128)S(1)} %get-tuple-element.11.pgrad), custom_call_target="tpu_custom_call" | custom-call | tf_op jit(solution)/shard_map/gather_out/pallas_call | solution.py:403
  93.5 0.8 copy.18
  94.3 0.8 copy.19
  95.1 0.7 copy.20
  95.8 0.7 copy.21
Async XLA Ops:
  0.6 21.9 %copy-start.7 = (s32[1,2]{1,0:T(1,128)S(1)}, s32[1,2]{1,0:T(1,128)}, u32[]{:S(2)}) copy-start(s32[1,2]{1,0:T(1,128)} %counts.1) | copy-start | bytes 28
  1.4 1.9 %copy-start = (f32[1,1,12,256,256]{4,3,2,1,0:T(8,128)S(1)}, f32[1,1,12,256,256]{4,3,2,1,0:T(8,128)}, u32[]{:S(2)}) copy-start(f32[1,1,12,256,256]{4,3,2,1,0:T(8,128)} %amp.1) | copy-start | bytes 9437188
  3.3 1.0 %copy-start.2 = (f32[512,256]{1,0:T(8,128)S(1)}, f32[512,256]{1,0:T(8,128)}, u32[]{:S(2)}) copy-start(f32[512,256]{1,0:T(8,128)} %obj_re.1) | copy-start | bytes 1572868
  4.4 1.0 %copy-start.3 = (f32[512,256]{1,0:T(8,128)S(1)}, f32[512,256]{1,0:T(8,128)}, u32[]{:S(2)}) copy-start(f32[512,256]{1,0:T(8,128)} %obj_im.1) | copy-start | bytes 1572868
  5.4 0.9 copy-start.6
  6.3 16.2 %copy-start.1 = (bf16[2,4,256,256]{3,2,1,0:T(8,128)(2,1)S(1)}, bf16[2,4,256,256]{3,2,1,0:T(8,128)(2,1)}, u32[]{:S(2)}) copy-start(bf16[2,4,256,256]{3,2,1,0:T(8,128)(2,1)} %constant.4.clone.tables) | copy-start | bytes 3145732
  6.3 16.3 %copy-start.4 = (f32[256,256]{1,0:T(8,128)S(1)}, f32[256,256]{1,0:T(8,128)}, u32[]{:S(2)}) copy-start(f32[256,256]{1,0:T(8,128)} %probe_re.1) | copy-start | bytes 786436
  6.3 16.3 %copy-start.5 = (f32[256,256]{1,0:T(8,128)S(1)}, f32[256,256]{1,0:T(8,128)}, u32[]{:S(2)}) copy-start(f32[256,256]{1,0:T(8,128)} %probe_im.1) | copy-start | bytes 786436

commit v2 on v1

v2 whole, which is shorter than its diff:
```python
import math

import jax
import jax.numpy as jnp
import ml_dtypes
import numpy as np
from jax import lax
from jax.experimental import pallas as pl
from jax.experimental.pallas import tpu as pltpu
from jax.sharding import PartitionSpec as P

N = 256
H = 128
TR = 512
SLOTS = 12
NTX = 128
ROWS = TR + N
MESH = pl.DeviceIdType.MESH
F32 = jnp.float32
BF16 = jnp.bfloat16


def half_dft_tables():
    n = np.arange(H, dtype=np.float64)[:, None]
    k = np.arange(H, dtype=np.float64)[None, :]
    tables = []
    for odd in (0, 1):
        angle = -2.0 * math.pi * (n * (2 * k + odd)) / N
        re, im = np.cos(angle) / 16.0, np.sin(angle) / 16.0
        tables.append(np.block([[re, im], [-im, re]]))
    both = np.stack([tables[0], tables[1], tables[0].T, tables[1].T])
    high = both.astype(ml_dtypes.bfloat16)
    low = (both - high.astype(np.float64)).astype(ml_dtypes.bfloat16)
    return np.stack([high, low])


def split(x):
    high = x.astype(BF16)
    return high, (x - high.astype(F32)).astype(BF16)


def dot(a, b):
    return jnp.dot(a, b, preferred_element_type=F32)


def halo_kernel(
    obj_re, obj_im, amp, reg, amp_out, raw, perm, sorted_amp,
    ty_send, ty_recv, up_send, up_recv, diag_send, diag_recv, own_sem, raw_sem, amp_sem,
):
    tx, ty = lax.axis_index("tx"), lax.axis_index("ty")
    up, down = lax.rem(tx + NTX - 1, NTX), lax.rem(tx + 1, NTX)
    partner = (tx, 1 - ty)
    barrier = pltpu.get_barrier_semaphore()
    for device in (partner, (up, ty), (down, ty)):
        pl.semaphore_signal(barrier, inc=1, device_id=device, device_id_type=MESH)
    raw_copies = []
    for t in range(2):
        c = pltpu.make_async_copy(amp.at[0, 0, :, :, pl.ds(t * H, H)], raw.at[t], raw_sem.at[t])
        c.start()
        raw_copies.append(c)
    own = []
    for p, obj in enumerate((obj_re, obj_im)):
        for t in range(2):
            c = pltpu.make_async_copy(
                obj.at[:, pl.ds(t * H, H)], reg.at[p, ty + t, pl.ds(0, TR)], own_sem.at[p, t])
            c.start()
            own.append(c)
    i, j = (lax.broadcasted_iota(jnp.int32, (N, N), d) for d in range(2))
    perm[...] = jnp.where(i == jnp.where(j < H, 2 * j, 2 * (j - H) + 1), 1.0, 0.0).astype(BF16)
    pl.semaphore_wait(barrier, 3)

    edge = pl.multiple_of((1 - ty) * H, H)
    across = [[], []]
    for half in range(2):
        for p, obj in enumerate((obj_re, obj_im)):
            rows = pl.ds(half * N, N)
            c = pltpu.make_async_remote_copy(
                src_ref=obj.at[rows, pl.ds(edge, H)], dst_ref=reg.at[p, 2 * ty, rows],
                send_sem=ty_send.at[half, p], recv_sem=ty_recv.at[half, p],
                device_id=partner, device_id_type=MESH)
            c.start()
            across[half].append(c)
    below = []
    for p, obj in enumerate((obj_re, obj_im)):
        for t in range(2):
            c = pltpu.make_async_remote_copy(
                src_ref=obj.at[pl.ds(0, N), pl.ds(t * H, H)], dst_ref=reg.at[p, ty + t, pl.ds(TR, N)],
                send_sem=up_send.at[p, t], recv_sem=up_recv.at[p, t],
                device_id=(up, ty), device_id_type=MESH)
            c.start()
            below.append(c)
    for c in raw_copies:
        c.wait()

    def sort_slot(i, carry):
        for h in range(2):
            rows = [raw[t, i, pl.ds(h, H, stride=2), :] for t in range(2)]
            high, low = split(jnp.concatenate(rows, axis=1))
            sorted_amp[i, pl.ds(h * H, H), :] = dot(high, perm[...]) + dot(low, perm[...])
        pltpu.make_async_copy(sorted_amp.at[i], amp_out.at[i], amp_sem.at[i]).start()
        return carry

    lax.fori_loop(0, SLOTS // 2, sort_slot, 0)
    diag = []
    for p in range(2):
        across[0][p].wait()
        side = 2 - 2 * ty
        c = pltpu.make_async_remote_copy(
            src_ref=reg.at[p, side, pl.ds(0, N)], dst_ref=reg.at[p, side, pl.ds(TR, N)],
            send_sem=diag_send.at[p], recv_sem=diag_recv.at[p],
            device_id=(up, ty), device_id_type=MESH)
        c.start()
        diag.append(c)
    lax.fori_loop(SLOTS // 2, SLOTS, sort_slot, 0)

    def finish_slot(i, carry):
        pltpu.make_async_copy(sorted_amp.at[i], amp_out.at[i], amp_sem.at[i]).wait()
        return carry

    lax.fori_loop(0, SLOTS, finish_slot, 0)
    for c in own + across[1] + below + diag:
        c.wait()


def halo(obj_re, obj_im, amp):
    anywhere = pl.BlockSpec(memory_space=pl.ANY)
    hbm = pl.BlockSpec(memory_space=pltpu.HBM)
    dma = pltpu.SemaphoreType.DMA
    return pl.pallas_call(
        halo_kernel,
        out_shape=(
            jax.ShapeDtypeStruct((2, 3, ROWS, H), F32),
            jax.ShapeDtypeStruct((SLOTS, N, N), F32),
        ),
        in_specs=[hbm, hbm, hbm],
        out_specs=(anywhere, anywhere),
        scratch_shapes=[
            pltpu.VMEM((2, SLOTS, N, H), F32),
            pltpu.VMEM((N, N), BF16),
            pltpu.VMEM((SLOTS, N, N), F32),
            dma((2, 2)), dma((2, 2)), dma((2, 2)), dma((2, 2)), dma((2,)), dma((2,)),
            dma((2, 2)), dma((2,)), dma((SLOTS,)),
        ],
        compiler_params=pltpu.CompilerParams(
            collective_id=0, has_side_effects=True, vmem_limit_bytes=58 << 20),
        name="halo",
    )(obj_re, obj_im, amp)


def positions_kernel(
    offsets, counts, reg, probe_re, probe_im, tables, amp_in, grad, pgrad,
    amp, win, sp, mid, amp_sem,
):
    tx, ty = lax.axis_index("tx"), lax.axis_index("ty")
    live = counts[0, ty]
    probe = (probe_re, probe_im)
    CH = 32

    def fetch(i):
        return pltpu.make_async_copy(amp_in.at[i], amp.at[i], amp_sem.at[i])

    def start_fetch(i, carry):
        fetch(i).start()
        return carry

    lax.fori_loop(0, live, start_fetch, 0)
    grad[...] = jnp.zeros_like(grad)
    pgrad[...] = jnp.zeros_like(pgrad)
    lane = lax.broadcasted_iota(jnp.int32, (CH, H), 1)

    def put(s, q, rows, lanes, value):
        high, low = split(value)
        sp[s, 0, q, rows, lanes] = high
        sp[s, 1, q, rows, lanes] = low

    def right(s, q, which):
        high, low = sp[s, 0, q], sp[s, 1, q]
        mid[s, q] = dot(jnp.concatenate([high, low, high], axis=1),
                        jnp.concatenate([tables[0, which], tables[0, which], tables[1, which]], axis=0))

    def left(s, q, which):
        high, low = sp[s, 0, q], sp[s, 1, q]
        mid[s, q] = dot(jnp.concatenate([tables[0, which], tables[1, which], tables[0, which]], axis=1),
                        jnp.concatenate([high, high, low], axis=0))

    def lanes(t):
        return pl.ds(t * H, H)

    def enter(s, place):
        row_at, col_at = place
        back = lax.rem(H - col_at, H)
        from_next = lane >= H - col_at
        for j in range(N // CH):
            rows = pl.ds(j * CH, CH)
            ex = [[None, None], [None, None]]
            w = [[None, None], [None, None]]
            for p in range(2):
                turned = [pltpu.roll(reg[p, t, pl.ds(row_at + j * CH, CH), :], back, 1) for t in range(3)]
                for t in range(2):
                    w[p][t] = jnp.where(from_next, turned[t + 1], turned[t])
                    win[s, p, t, rows, :] = w[p][t]
            for t in range(2):
                pr, pi = probe_re[rows, lanes(t)], probe_im[rows, lanes(t)]
                ex[0][t] = pr * w[0][t] - pi * w[1][t]
                ex[1][t] = pr * w[1][t] + pi * w[0][t]
            for p in range(2):
                put(s, 0, rows, lanes(p), ex[p][0] + ex[p][1])
                put(s, 1, rows, lanes(p), ex[p][0] - ex[p][1])

    def fold_rows(s):
        for j in range(H // CH):
            for q in range(2):
                for p in range(2):
                    top = mid[s, q, pl.ds(j * CH, CH), lanes(p)]
                    low = mid[s, q, pl.ds(H + j * CH, CH), lanes(p)]
                    rows = pl.ds(p * H + j * CH, CH)
                    put(s, 0, rows, lanes(q), top + low)
                    put(s, 1, rows, lanes(q), top - low)

    def compare(s, i, used):
        for j in range(H // CH):
            for h in range(2):
                rows_re, rows_im = pl.ds(j * CH, CH), pl.ds(H + j * CH, CH)
                re, im = mid[s, h, rows_re, :], mid[s, h, rows_im, :]
                measured = amp[i, pl.ds(h * H + j * CH, CH), :]
                keep = 1.0 - measured * lax.rsqrt(jnp.maximum(re * re + im * im, 1.0))
                keep = jnp.where(used, keep, 0.0)
                put(s, h, rows_re, slice(None), re * keep)
                put(s, h, rows_im, slice(None), im * keep)

    def unfold_rows(s):
        for j in range(H // CH):
            for p in range(2):
                for q in range(2):
                    a = mid[s, 0, pl.ds(p * H + j * CH, CH), lanes(q)]
                    b = mid[s, 1, pl.ds(p * H + j * CH, CH), lanes(q)]
                    put(s, q, pl.ds(j * CH, CH), lanes(p), a + b)
                    put(s, q, pl.ds(H + j * CH, CH), lanes(p), a - b)

    def leave(s, place):
        row_at, col_at = place
        ahead = lax.rem(col_at, H)
        to_next = lane < col_at
        for j in range(N // CH):
            rows = pl.ds(j * CH, CH)
            g = [[None, None], [None, None]]
            for t in range(2):
                chi = []
                for p in range(2):
                    a, b = mid[s, 0, rows, lanes(p)], mid[s, 1, rows, lanes(p)]
                    chi.append(a + b if t == 0 else a - b)
                pr, pi = probe_re[rows, lanes(t)], probe_im[rows, lanes(t)]
                wr, wi = win[s, 0, t, rows, :], win[s, 1, t, rows, :]
                g[0][t] = pltpu.roll(pr * chi[0] + pi * chi[1], ahead, 1)
                g[1][t] = pltpu.roll(pr * chi[1] - pi * chi[0], ahead, 1)
                pgrad[0, t, rows, :] += wr * chi[0] + wi * chi[1]
                pgrad[1, t, rows, :] += wr * chi[1] - wi * chi[0]
            at = pl.ds(row_at + j * CH, CH)
            for p in range(2):
                grad[p, 0, at, :] += jnp.where(to_next, 0.0, g[p][0])
                grad[p, 1, at, :] += jnp.where(to_next, g[p][0], g[p][1])
                grad[p, 2, at, :] += jnp.where(to_next, g[p][1], 0.0)

    def place_of(i):
        return offsets[0, ty, 0, i] - tx * TR, offsets[0, ty, 1, i] - ty * H

    def pair(k, carry):
        ids = [2 * k, jnp.minimum(2 * k + 1, live - 1)]
        used = [True, 2 * k + 1 < live]
        places = [place_of(i) for i in ids]
        fetch(ids[0]).wait()

        @pl.when(used[1])
        def _():
            fetch(ids[1]).wait()

        steps = [
            lambda s: enter(s, places[s]),
            lambda s: [right(s, q, q) for q in range(2)],
            lambda s: fold_rows(s),
            lambda s: [left(s, h, 2 + h) for h in range(2)],
            lambda s: compare(s, ids[s], used[s]),
            lambda s: [left(s, h, h) for h in range(2)],
            lambda s: unfold_rows(s),
            lambda s: [right(s, q, 2 + q) for q in range(2)],
            lambda s: leave(s, places[s]),
        ]
        steps[0](0)
        for n in range(1, len(steps)):
            steps[n](0)
            steps[n - 1](1)
        steps[-1](1)
        return carry

    lax.fori_loop(0, (live + 1) // 2, pair, 0)


def positions(offsets, counts, reg, probe_re, probe_im, tables, amp):
    smem = pl.BlockSpec(memory_space=pltpu.SMEM)
    vmem = pl.BlockSpec(memory_space=pltpu.VMEM)
    return pl.pallas_call(
        positions_kernel,
        out_shape=(
            jax.ShapeDtypeStruct((2, 3, ROWS, H), F32),
            jax.ShapeDtypeStruct((2, 2, N, H), F32),
        ),
        in_specs=[smem, smem, vmem, vmem, vmem, vmem, pl.BlockSpec(memory_space=pl.ANY)],
        out_specs=(vmem, vmem),
        scratch_shapes=[
            pltpu.VMEM((SLOTS, N, N), F32),
            pltpu.VMEM((2, 2, 2, N, H), F32),
            pltpu.VMEM((2, 2, 2, N, N), BF16),
            pltpu.VMEM((2, 2, N, N), F32),
            pltpu.SemaphoreType.DMA((SLOTS,)),
        ],
        compiler_params=pltpu.CompilerParams(vmem_limit_bytes=46 << 20),
        name="positions",
    )(offsets, counts, reg, probe_re, probe_im, tables, amp)


def out_kernel(
    grad, pgrad, out_ty, out_up, out_full, out_other,
    came_diag, edge, core_in, acc, xy_in, z_all,
    ty_send, ty_recv, up_send, up_recv, diag_send, diag_recv,
    core_send, core_recv, xy_send, xy_recv, z_send, z_recv,
):
    tx, ty = lax.axis_index("tx"), lax.axis_index("ty")
    up, down = lax.rem(tx + NTX - 1, NTX), lax.rem(tx + 1, NTX)
    partner = (tx, 1 - ty)
    core, y, z, x_lo = lax.rem(tx, 2), lax.rem(tx // 2, 4), lax.rem(tx // 8, 8), tx // 64
    x = ty * 2 + x_lo

    def at(core_, y_, z_, x_):
        return (((lax.rem(x_, 2) * 8 + z_) * 4 + y_) * 2 + core_, x_ // 2)

    core_mate = at(1 - core, y, z, x)
    steps = [(i, j) for i in range(4) for j in range(4) if i or j]
    steps.sort(key=lambda s: -(min(s[0], 4 - s[0]) + min(s[1], 4 - s[1])))
    xy_at = [(lax.rem(y + i, 4), lax.rem(x + j, 4)) for i, j in steps]
    xy_mates = [at(core, y_, z, x_) for y_, x_ in xy_at]
    z_mates = [at(core, y, lax.rem(z + d, 8), x) for d in (4, 3, 5, 2, 6, 1, 7)]
    greeted = [partner, (up, ty), (down, ty), core_mate] + xy_mates + z_mates
    barrier = pltpu.get_barrier_semaphore()
    for device in greeted:
        pl.semaphore_signal(barrier, inc=1, device_id=device, device_id_type=MESH)
    pl.semaphore_wait(barrier, len(greeted))

    def send(src, dst, send_sem, recv_sem, device):
        c = pltpu.make_async_remote_copy(
            src_ref=src, dst_ref=dst, send_sem=send_sem, recv_sem=recv_sem,
            device_id=device, device_id_type=MESH)
        c.start()
        return c

    def part(i, j):
        return pl.ds(pl.multiple_of((i * 4 + j) * 32, 32), 32)

    side = 2 - 2 * ty
    core_copy = send(pgrad.at[1 - core], core_in, core_send.at[0], core_recv.at[0], core_mate)
    diag = send(grad.at[:, side, pl.ds(TR, N)], came_diag, diag_send, diag_recv, (down, ty))
    core_copy.wait()
    for t in range(2):
        acc[pl.ds(t * N, N), :] = pgrad[core, t] + core_in[t]
    xy_copies = [
        send(acc.at[part(*xy_at[d])], xy_in.at[d], xy_send.at[0, d], xy_recv.at[0, d], xy_mates[d])
        for d in range(15)]

    for c in xy_copies:
        c.wait()
    total = acc[part(y, x), :]
    for d in range(15):
        total = total + xy_in[d]
    z_all[z] = total
    z_copies = [
        send(z_all.at[z], z_all.at[z], z_send.at[d], z_recv.at[d], z_mates[d]) for d in range(7)]
    far_rows = send(
        grad.at[:, side, pl.ds(N, N)], out_ty.at[:, pl.ds(N, N)], ty_send.at[1], ty_recv.at[1], partner)
    below = send(grad.at[:, pl.ds(ty, 2), pl.ds(TR, N)], out_up, up_send, up_recv, (down, ty))
    diag.wait()
    for p in range(2):
        edge[p] = grad[p, side, pl.ds(0, N)] + came_diag[p]
    near_rows = send(edge, out_ty.at[:, pl.ds(0, N)], ty_send.at[0], ty_recv.at[0], partner)

    for c in z_copies:
        c.wait()
    total = z_all[0]
    for d in range(1, 8):
        total = total + z_all[d]
    out_full[part(y, x), :] = total * (1.0 / (NTX * 2 * SLOTS))
    xy_copies = [
        send(out_full.at[part(y, x)], out_full.at[part(y, x)], xy_send.at[1, d], xy_recv.at[1, d], xy_mates[d])
        for d in range(15)]

    for c in xy_copies:
        c.wait()
    core_copy = send(out_full, out_other, core_send.at[1], core_recv.at[1], core_mate)
    below.wait()
    far_rows.wait()
    near_rows.wait()
    core_copy.wait()


def finish_kernel(grad, came_ty, came_up, full, other, out_re, out_im, pout_re, pout_im):
    core, ty = lax.rem(lax.axis_index("tx"), 2), lax.axis_index("ty")
    for p, out in enumerate((out_re, out_im)):
        for t in range(2):
            lanes = pl.ds(t * H, H)
            mine = ty == 1 - t
            ty_rows = [jnp.where(mine, came_ty[p, pl.ds(h * N, N)], 0.0) for h in range(2)]
            out[pl.ds(0, N), lanes] = grad[p, ty + t, pl.ds(0, N)] + came_up[p, t] + ty_rows[0]
            out[pl.ds(N, N), lanes] = grad[p, ty + t, pl.ds(N, N)] + ty_rows[1]
    for t in range(2):
        rows, lanes = pl.ds(t * N, N), pl.ds(t * H, H)
        a, b = full[rows, :], other[rows, :]
        pout_re[:, lanes] = jnp.where(core == 0, a, b)
        pout_im[:, lanes] = jnp.where(core == 0, b, a)


def gather_out(grad, pgrad):
    vmem = pl.BlockSpec(memory_space=pltpu.VMEM)
    dma = pltpu.SemaphoreType.DMA
    tile = jax.ShapeDtypeStruct((TR, N), F32)
    patch = jax.ShapeDtypeStruct((N, N), F32)
    came = pl.pallas_call(
        out_kernel,
        out_shape=(
            jax.ShapeDtypeStruct((2, TR, H), F32),
            jax.ShapeDtypeStruct((2, 2, N, H), F32),
            jax.ShapeDtypeStruct((2 * N, H), F32),
            jax.ShapeDtypeStruct((2 * N, H), F32),
        ),
        in_specs=[vmem, vmem],
        out_specs=(vmem, vmem, vmem, vmem),
        scratch_shapes=[
            pltpu.VMEM((2, N, H), F32),
            pltpu.VMEM((2, N, H), F32),
            pltpu.VMEM((2, N, H), F32),
            pltpu.VMEM((2 * N, H), F32),
            pltpu.VMEM((15, 32, H), F32),
            pltpu.VMEM((8, 32, H), F32),
            dma((2,)), dma((2,)), dma(()), dma(()), dma(()), dma(()),
            dma((2,)), dma((2,)), dma((2, 15)), dma((2, 15)), dma((7,)), dma((7,)),
        ],
        compiler_params=pltpu.CompilerParams(
            collective_id=1, has_side_effects=True, vmem_limit_bytes=20 << 20),
        name="gather_out",
    )(grad, pgrad)
    return pl.pallas_call(
        finish_kernel,
        out_shape=(tile, tile, patch, patch),
        in_specs=[vmem] * 5,
        out_specs=(vmem,) * 4,
        compiler_params=pltpu.CompilerParams(vmem_limit_bytes=20 << 20),
        name="finish",
    )(grad, *came)


def per_device(obj_re, obj_im, probe_re, probe_im, amplitude, offsets, counts):
    tables = jnp.asarray(half_dft_tables())
    reg, amp = halo(obj_re, obj_im, amplitude)
    grad, pgrad = positions(jnp.swapaxes(offsets, 2, 3), counts, reg, probe_re, probe_im, tables, amp)
    return gather_out(grad, pgrad)


def solution(mesh):
    return jax.shard_map(
        per_device,
        mesh=mesh,
        in_specs=(
            P("tx", "ty"),
            P("tx", "ty"),
            P(),
            P(),
            P("tx", "ty", None, None, None),
            P("tx", None, None, None),
            P("tx", None),
        ),
        out_specs=(P("tx", "ty"), P("tx", "ty"), P(), P()),
        check_vma=False,
    )
```

time: 96.8 us -> 95.1 us (0.982)
  local copies, waits for them, and re-layouts: 8.66 us -> 1.68 us
  Pallas kernels: 87.1 us -> 92.5 us
    pallas_call x1, Pallas kernels: 16.2 us -> 33.4 us  [halo(): pl.pallas_call(halo_kernel, out_shape=(jax.ShapeDtypeStruct((2, 3, ROWS,...]
    pallas_call x1 -> x2, Pallas kernels: 61.4 us -> 49.7 us  [the longest x1 48.4 us: gather_out(): pl.pallas_call(out_kernel, out_shape=(jax.ShapeDtypeStruct((2, TR, H), F3...]
    unnamed x21 -> x12, local copies, waits for them, and re-layouts: 8.66 us -> 1.68 us
where the time goes in v2:
time: 95.1 us; the launch traced here: 94.9 us
  Pallas kernels  92.5 us (97%)
  local copies, waits for them, and re-layouts  1.68 us (2%)
    pallas_call x1, Pallas kernels, gather_out(): pl.pallas_call(out_kernel, out_shape=(jax.ShapeDtypeStruct((2, TR, H), F3...  48.4 us
    pallas_call x1, Pallas kernels, halo(): pl.pallas_call(halo_kernel, out_shape=(jax.ShapeDtypeStruct((2, 3, ROWS,...  33.4 us
    pallas_call x1, Pallas kernels, positions(): pl.pallas_call(positions_kernel, out_shape=(jax.ShapeDtypeStruct((2, 3, R...  9.36 us

profile of v2, /device:TPU:1, one launch (start us, length us, event | category | flops | bytes accessed | tf_op | source)
XLA Modules:
  0.0 94.9 jit_solution(7451829839014305401)
XLA Ops:
  0.6 0.0 copy-start.1
  0.6 0.0 copy-start.5
  0.7 0.0 copy-start.4
  0.7 0.0 copy-start.3
  0.7 0.0 copy-start.2
  0.7 33.4 %halo.1 = (f32[2,3,768,128]{3,2,1,0:T(8,128)}, f32[12,256,256]{2,1,0:T(8,128)}) custom-call(f32[512,256]{1,0:T(8,128)} %obj_re.1, f32[512,256]{1,0:T(8,128)} %obj_im.1, f32[1,1,12,256,256]{4,3,2,1,0:T(8,128)} %amp.1), custom_call_target="tpu_custom_call" | custom-call | tf_op jit(solution)/shard_map/halo/pallas_call | solution.py:129
  34.1 0.0 copy-done.1
  34.1 0.0 copy-done.5
  34.1 0.0 copy-done.4
  34.1 0.0 copy-done.3
  34.1 0.0 copy-done.2
  34.1 0.0 copy-start
  34.2 1.7 %copy-done = f32[2,3,768,128]{3,2,1,0:T(8,128)S(1)} copy-done((f32[2,3,768,128]{3,2,1,0:T(8,128)S(1)}, f32[2,3,768,128]{3,2,1,0:T(8,128)}, u32[]{:S(2)}) %copy-start) | copy-done | bytes 2359320
  35.8 9.4 %positions.1 = (f32[2,3,768,128]{3,2,1,0:T(8,128)S(1)}, f32[2,2,256,128]{3,2,1,0:T(8,128)S(1)}) custom-call(s32[1,2,2,12]{3,2,1,0:T(2,128)S(1)} %bitcast.1, s32[1,2]{1,0:T(1,128)S(1)} %copy-done.5, f32[2,3,768,128]{3,2,1,0:T(8,128)S(1)} %copy-done, f32[256,256]{1,0:T(8,128)S(1)} %copy-done.2, f32[256,256]{1,0:T(8,128)S(1)} %copy-done.3, ...), custom_call_target="tpu_custom_call" | custom-call | tf_op jit(solution)/shard_map/positions/pallas_call | solution.py:301
  45.2 48.4 %gather_out.1 = (f32[2,512,128]{2,1,0:T(8,128)S(1)}, f32[2,2,256,128]{3,2,1,0:T(8,128)S(1)}, f32[512,128]{1,0:T(8,128)S(1)}, f32[512,128]{1,0:T(8,128)S(1)}) custom-call(f32[2,3,768,128]{3,2,1,0:T(8,128)S(1)} %get-tuple-element.14.grad, f32[2,2,256,128]{3,2,1,0:T(8,128)S(1)} %get-tuple-element.15.pgrad), custom_call_target="tpu_custom_call" | custom-call | tf_op jit(solution)/shard_map/gather_out/pallas_call | solution.py:424
  93.6 1.3 %finish.1 = (f32[512,256]{1,0:T(8,128)}, f32[512,256]{1,0:T(8,128)}, f32[256,256]{1,0:T(8,128)}, f32[256,256]{1,0:T(8,128)}) custom-call(f32[2,3,768,128]{3,2,1,0:T(8,128)S(1)} %get-tuple-element.14.grad, f32[2,512,128]{2,1,0:T(8,128)S(1)} %get-tuple-element.16.came_ty, f32[2,2,256,128]{3,2,1,0:T(8,128)S(1)} %get-tuple-element.17.came_up, ...), custom_call_target="tpu_custom_call" | custom-call | tf_op jit(solution)/shard_map/finish/pallas_call | solution.py:448
Async XLA Ops:
  0.6 33.5 %copy-start.1 = (bf16[2,4,256,256]{3,2,1,0:T(8,128)(2,1)S(1)}, bf16[2,4,256,256]{3,2,1,0:T(8,128)(2,1)}, u32[]{:S(2)}) copy-start(bf16[2,4,256,256]{3,2,1,0:T(8,128)(2,1)} %constant.2.clone.tables) | copy-start | bytes 3145732
  0.6 33.5 %copy-start.5 = (s32[1,2]{1,0:T(1,128)S(1)}, s32[1,2]{1,0:T(1,128)}, u32[]{:S(2)}) copy-start(s32[1,2]{1,0:T(1,128)} %counts.1) | copy-start | bytes 28
  0.7 33.5 %copy-start.4 = (s32[1,2,12,2]{2,3,1,0:T(2,128)S(1)}, s32[1,2,12,2]{2,3,1,0:T(2,128)}, u32[]{:S(2)}) copy-start(s32[1,2,12,2]{2,3,1,0:T(2,128)} %param.13) | copy-start | bytes 580
  0.7 33.5 %copy-start.3 = (f32[256,256]{1,0:T(8,128)S(1)}, f32[256,256]{1,0:T(8,128)}, u32[]{:S(2)}) copy-start(f32[256,256]{1,0:T(8,128)} %probe_im.1) | copy-start | bytes 786436
  0.7 33.5 %copy-start.2 = (f32[256,256]{1,0:T(8,128)S(1)}, f32[256,256]{1,0:T(8,128)}, u32[]{:S(2)}) copy-start(f32[256,256]{1,0:T(8,128)} %probe_re.1) | copy-start | bytes 786436
  34.1 1.7 %copy-start = (f32[2,3,768,128]{3,2,1,0:T(8,128)S(1)}, f32[2,3,768,128]{3,2,1,0:T(8,128)}, u32[]{:S(2)}) copy-start(f32[2,3,768,128]{3,2,1,0:T(8,128)} %get-tuple-element.12.reg) | copy-start | bytes 7077892

commit v3 on v2

--- a/solution.py
+++ b/solution.py
@@ -44,8 +44,8 @@
 
 
 def halo_kernel(
-    obj_re, obj_im, amp, reg, amp_out, raw, perm, sorted_amp,
-    ty_send, ty_recv, up_send, up_recv, diag_send, diag_recv, own_sem, raw_sem, amp_sem,
+    obj_re, obj_im, amp, reg, amp_out, raw, perm,
+    ty_send, ty_recv, up_send, up_recv, diag_send, diag_recv, own_sem, raw_sem,
 ):
     tx, ty = lax.axis_index("tx"), lax.axis_index("ty")
     up, down = lax.rem(tx + NTX - 1, NTX), lax.rem(tx + 1, NTX)
@@ -96,8 +96,7 @@
         for h in range(2):
             rows = [raw[t, i, pl.ds(h, H, stride=2), :] for t in range(2)]
             high, low = split(jnp.concatenate(rows, axis=1))
-            sorted_amp[i, pl.ds(h * H, H), :] = dot(high, perm[...]) + dot(low, perm[...])
-        pltpu.make_async_copy(sorted_amp.at[i], amp_out.at[i], amp_sem.at[i]).start()
+            amp_out[i, pl.ds(h * H, H), :] = dot(high, perm[...]) + dot(low, perm[...])
         return carry
 
     lax.fori_loop(0, SLOTS // 2, sort_slot, 0)
@@ -113,57 +112,41 @@
         diag.append(c)
     lax.fori_loop(SLOTS // 2, SLOTS, sort_slot, 0)
 
-    def finish_slot(i, carry):
-        pltpu.make_async_copy(sorted_amp.at[i], amp_out.at[i], amp_sem.at[i]).wait()
-        return carry
-
-    lax.fori_loop(0, SLOTS, finish_slot, 0)
     for c in own + across[1] + below + diag:
         c.wait()
 
 
 def halo(obj_re, obj_im, amp):
-    anywhere = pl.BlockSpec(memory_space=pl.ANY)
-    hbm = pl.BlockSpec(memory_space=pltpu.HBM)
+    hbm, vmem = (pl.BlockSpec(memory_space=m) for m in (pltpu.HBM, pltpu.VMEM))
     dma = pltpu.SemaphoreType.DMA
     return pl.pallas_call(
         halo_kernel,
         out_shape=(
-            jax.ShapeDtypeStruct((2, 3, ROWS, H), F32),
-            jax.ShapeDtypeStruct((SLOTS, N, N), F32),
+            pltpu.VMEM((2, 3, ROWS, H), F32),
+            pltpu.VMEM((SLOTS, N, N), F32),
         ),
         in_specs=[hbm, hbm, hbm],
-        out_specs=(anywhere, anywhere),
+        out_specs=(vmem, vmem),
         scratch_shapes=[
             pltpu.VMEM((2, SLOTS, N, H), F32),
             pltpu.VMEM((N, N), BF16),
-            pltpu.VMEM((SLOTS, N, N), F32),
             dma((2, 2)), dma((2, 2)), dma((2, 2)), dma((2, 2)), dma((2,)), dma((2,)),
-            dma((2, 2)), dma((2,)), dma((SLOTS,)),
+            dma((2, 2)), dma((2,)),
         ],
         compiler_params=pltpu.CompilerParams(
-            collective_id=0, has_side_effects=True, vmem_limit_bytes=58 << 20),
+            collective_id=0, has_side_effects=True, vmem_limit_bytes=20 << 20),
         name="halo",
-    )(obj_re, obj_im, amp)
+    )(*(pltpu.with_memory_space_constraint(x, pltpu.HBM) for x in (obj_re, obj_im, amp)))
 
 
 def positions_kernel(
-    offsets, counts, reg, probe_re, probe_im, tables, amp_in, grad, pgrad,
-    amp, win, sp, mid, amp_sem,
+    offsets, counts, reg, probe_re, probe_im, tables, amp, grad, pgrad, win, sp, mid,
 ):
     tx, ty = lax.axis_index("tx"), lax.axis_index("ty")
     live = counts[0, ty]
     probe = (probe_re, probe_im)
     CH = 32
 
-    def fetch(i):
-        return pltpu.make_async_copy(amp_in.at[i], amp.at[i], amp_sem.at[i])
-
-    def start_fetch(i, carry):
-        fetch(i).start()
-        return carry
-
-    lax.fori_loop(0, live, start_fetch, 0)
     grad[...] = jnp.zeros_like(grad)
     pgrad[...] = jnp.zeros_like(pgrad)
     lane = lax.broadcasted_iota(jnp.int32, (CH, H), 1)
@@ -268,12 +251,6 @@
         ids = [2 * k, jnp.minimum(2 * k + 1, live - 1)]
         used = [True, 2 * k + 1 < live]
         places = [place_of(i) for i in ids]
-        fetch(ids[0]).wait()
-
-        @pl.when(used[1])
-        def _():
-            fetch(ids[1]).wait()
-
         steps = [
             lambda s: enter(s, places[s]),
             lambda s: [right(s, q, q) for q in range(2)],
@@ -301,28 +278,26 @@
     return pl.pallas_call(
         positions_kernel,
         out_shape=(
-            jax.ShapeDtypeStruct((2, 3, ROWS, H), F32),
-            jax.ShapeDtypeStruct((2, 2, N, H), F32),
+            pltpu.VMEM((2, 3, ROWS, H), F32),
+            pltpu.VMEM((2, 2, N, H), F32),
         ),
-        in_specs=[smem, smem, vmem, vmem, vmem, vmem, pl.BlockSpec(memory_space=pl.ANY)],
+        in_specs=[smem, smem, vmem, vmem, vmem, vmem, vmem],
         out_specs=(vmem, vmem),
         scratch_shapes=[
-            pltpu.VMEM((SLOTS, N, N), F32),
             pltpu.VMEM((2, 2, 2, N, H), F32),
             pltpu.VMEM((2, 2, 2, N, N), BF16),
             pltpu.VMEM((2, 2, N, N), F32),
-            pltpu.SemaphoreType.DMA((SLOTS,)),
         ],
-        compiler_params=pltpu.CompilerParams(vmem_limit_bytes=46 << 20),
+        compiler_params=pltpu.CompilerParams(vmem_limit_bytes=20 << 20),
         name="positions",
     )(offsets, counts, reg, probe_re, probe_im, tables, amp)
 
 
 def out_kernel(
     grad, pgrad, out_ty, out_up, out_full, out_other,
-    came_diag, edge, core_in, acc, xy_in, z_all,
+    came_diag, edge, core_in, acc, yz_in, shared,
     ty_send, ty_recv, up_send, up_recv, diag_send, diag_recv,
-    core_send, core_recv, xy_send, xy_recv, z_send, z_recv,
+    core_send, core_recv, yz_send, yz_recv, far_send, far_recv,
 ):
     tx, ty = lax.axis_index("tx"), lax.axis_index("ty")
     up, down = lax.rem(tx + NTX - 1, NTX), lax.rem(tx + 1, NTX)
@@ -334,12 +309,14 @@
         return (((lax.rem(x_, 2) * 8 + z_) * 4 + y_) * 2 + core_, x_ // 2)
 
     core_mate = at(1 - core, y, z, x)
+    z_low, z_high = lax.rem(z, 4), z // 4
     steps = [(i, j) for i in range(4) for j in range(4) if i or j]
     steps.sort(key=lambda s: -(min(s[0], 4 - s[0]) + min(s[1], 4 - s[1])))
-    xy_at = [(lax.rem(y + i, 4), lax.rem(x + j, 4)) for i, j in steps]
-    xy_mates = [at(core, y_, z, x_) for y_, x_ in xy_at]
-    z_mates = [at(core, y, lax.rem(z + d, 8), x) for d in (4, 3, 5, 2, 6, 1, 7)]
-    greeted = [partner, (up, ty), (down, ty), core_mate] + xy_mates + z_mates
+    yz_at = [(lax.rem(y + i, 4), lax.rem(z_low + j, 4)) for i, j in steps]
+    yz_mates = [at(core, i, z_high * 4 + j, x) for i, j in yz_at]
+    hops = [(1, 2), (1, 1), (1, 3), (1, 0), (0, 2), (0, 1), (0, 3)]
+    far_mates = [at(core, y, lax.rem(z_high + i, 2) * 4 + z_low, lax.rem(x + j, 4)) for i, j in hops]
+    greeted = [partner, (up, ty), (down, ty), core_mate] + yz_mates + far_mates
     barrier = pltpu.get_barrier_semaphore()
     for device in greeted:
         pl.semaphore_signal(barrier, inc=1, device_id=device, device_id_type=MESH)
@@ -358,40 +335,39 @@
     side = 2 - 2 * ty
     core_copy = send(pgrad.at[1 - core], core_in, core_send.at[0], core_recv.at[0], core_mate)
     diag = send(grad.at[:, side, pl.ds(TR, N)], came_diag, diag_send, diag_recv, (down, ty))
+    far_rows = send(
+        grad.at[:, side, pl.ds(N, N)], out_ty.at[:, pl.ds(N, N)], ty_send.at[1], ty_recv.at[1], partner)
     core_copy.wait()
     for t in range(2):
         acc[pl.ds(t * N, N), :] = pgrad[core, t] + core_in[t]
-    xy_copies = [
-        send(acc.at[part(*xy_at[d])], xy_in.at[d], xy_send.at[0, d], xy_recv.at[0, d], xy_mates[d])
+    yz_copies = [
+        send(acc.at[part(*yz_at[d])], yz_in.at[d], yz_send.at[0, d], yz_recv.at[0, d], yz_mates[d])
         for d in range(15)]
-
-    for c in xy_copies:
-        c.wait()
-    total = acc[part(y, x), :]
-    for d in range(15):
-        total = total + xy_in[d]
-    z_all[z] = total
-    z_copies = [
-        send(z_all.at[z], z_all.at[z], z_send.at[d], z_recv.at[d], z_mates[d]) for d in range(7)]
-    far_rows = send(
-        grad.at[:, side, pl.ds(N, N)], out_ty.at[:, pl.ds(N, N)], ty_send.at[1], ty_recv.at[1], partner)
-    below = send(grad.at[:, pl.ds(ty, 2), pl.ds(TR, N)], out_up, up_send, up_recv, (down, ty))
     diag.wait()
     for p in range(2):
         edge[p] = grad[p, side, pl.ds(0, N)] + came_diag[p]
+    for c in yz_copies:
+        c.wait()
+    total = acc[part(y, z_low), :]
+    for d in range(15):
+        total = total + yz_in[d]
+    mine = x * 2 + z_high
+    shared[mine] = total
+    far_copies = [
+        send(shared.at[mine], shared.at[mine], far_send.at[d], far_recv.at[d], far_mates[d]) for d in range(7)]
+    below = send(grad.at[:, pl.ds(ty, 2), pl.ds(TR, N)], out_up, up_send, up_recv, (down, ty))
+    for c in far_copies:
+        c.wait()
+    total = shared[0]
+    for d in range(1, 8):
+        total = total + shared[d]
+    out_full[part(y, z_low), :] = total * (1.0 / (NTX * 2 * SLOTS))
+    yz_copies = [
+        send(out_full.at[part(y, z_low)], out_full.at[part(y, z_low)],
+             yz_send.at[1, d], yz_recv.at[1, d], yz_mates[d])
+        for d in range(15)]
     near_rows = send(edge, out_ty.at[:, pl.ds(0, N)], ty_send.at[0], ty_recv.at[0], partner)
-
-    for c in z_copies:
-        c.wait()
-    total = z_all[0]
-    for d in range(1, 8):
-        total = total + z_all[d]
-    out_full[part(y, x), :] = total * (1.0 / (NTX * 2 * SLOTS))
-    xy_copies = [
-        send(out_full.at[part(y, x)], out_full.at[part(y, x)], xy_send.at[1, d], xy_recv.at[1, d], xy_mates[d])
-        for d in range(15)]
-
-    for c in xy_copies:
+    for c in yz_copies:
         c.wait()
     core_copy = send(out_full, out_other, core_send.at[1], core_recv.at[1], core_mate)
     below.wait()

time: 95.1 us -> 78.7 us (0.83)
  Pallas kernels: 92.5 us -> 77.8 us
  local copies, waits for them, and re-layouts: 1.68 us -> 0.02 us
    pallas_call x2, Pallas kernels: 42.8 us -> 30.6 us  [the longest x1 16.5 us: halo(): pl.pallas_call(halo_kernel, out_shape=(pltpu.VMEM((2, 3, ROWS, H), F32),...]
    pallas_call x1, Pallas kernels: 48.4 us -> 45.9 us  [gather_out(): pl.pallas_call(out_kernel, out_shape=(jax.ShapeDtypeStruct((2, TR, H), F3...]
    unnamed x12 -> x10, local copies, waits for them, and re-layouts: 1.68 us -> 0.02 us
where the time goes in v3:
time: 78.7 us; the launch traced here: 78.6 us
  Pallas kernels  77.8 us (99%)
    pallas_call x1, Pallas kernels, gather_out(): pl.pallas_call(out_kernel, out_shape=(jax.ShapeDtypeStruct((2, TR, H), F3...  45.9 us
    pallas_call x1, Pallas kernels, halo(): pl.pallas_call(halo_kernel, out_shape=(pltpu.VMEM((2, 3, ROWS, H), F32),...  16.5 us
    pallas_call x1, Pallas kernels, positions(): pl.pallas_call(positions_kernel, out_shape=(pltpu.VMEM((2, 3, ROWS, H), F...  14.2 us

profile of v3, /device:TPU:1, one launch (start us, length us, event | category | flops | bytes accessed | tf_op | source)
XLA Modules:
  0.0 78.6 jit_solution(3248890470685611210)
XLA Ops:
  0.6 0.0 copy-start
  0.6 0.0 copy-start.4
  0.7 0.0 copy-start.3
  0.7 0.0 copy-start.2
  0.7 0.0 copy-start.1
  0.7 16.5 %halo.1 = (f32[2,3,768,128]{3,2,1,0:T(8,128)S(1)}, f32[12,256,256]{2,1,0:T(8,128)S(1)}) custom-call(f32[512,256]{1,0:T(8,128)} %obj_re.1, f32[512,256]{1,0:T(8,128)} %obj_im.1, f32[1,1,12,256,256]{4,3,2,1,0:T(8,128)} %amp.1), custom_call_target="tpu_custom_call" | custom-call | tf_op jit(solution)/shard_map/halo/pallas_call | solution.py:122
  17.2 0.0 copy-done
  17.2 0.0 copy-done.4
  17.2 0.0 copy-done.3
  17.2 0.0 copy-done.2
  17.2 0.0 copy-done.1
  17.2 14.2 %positions.1 = (f32[2,3,768,128]{3,2,1,0:T(8,128)S(1)}, f32[2,2,256,128]{3,2,1,0:T(8,128)S(1)}) custom-call(s32[1,2,2,12]{3,2,1,0:T(2,128)S(1)} %bitcast.1, s32[1,2]{1,0:T(1,128)S(1)} %copy-done.4, f32[2,3,768,128]{3,2,1,0:T(8,128)S(1)} %get-tuple-element.12.reg, f32[256,256]{1,0:T(8,128)S(1)} %copy-done.1, f32[256,256]{1,0:T(8,128)S(1)} %copy-done.2, ...), custom_call_target="tpu_custom_call" | custom-call | tf_op jit(solution)/shard_map/positions/pallas_call | solution.py:278
  31.4 45.9 %gather_out.1 = (f32[2,512,128]{2,1,0:T(8,128)S(1)}, f32[2,2,256,128]{3,2,1,0:T(8,128)S(1)}, f32[512,128]{1,0:T(8,128)S(1)}, f32[512,128]{1,0:T(8,128)S(1)}) custom-call(f32[2,3,768,128]{3,2,1,0:T(8,128)S(1)} %get-tuple-element.14.grad, f32[2,2,256,128]{3,2,1,0:T(8,128)S(1)} %get-tuple-element.15.pgrad), custom_call_target="tpu_custom_call" | custom-call | tf_op jit(solution)/shard_map/gather_out/pallas_call | solution.py:400
  77.2 1.3 %finish.1 = (f32[512,256]{1,0:T(8,128)}, f32[512,256]{1,0:T(8,128)}, f32[256,256]{1,0:T(8,128)}, f32[256,256]{1,0:T(8,128)}) custom-call(f32[2,3,768,128]{3,2,1,0:T(8,128)S(1)} %get-tuple-element.14.grad, f32[2,512,128]{2,1,0:T(8,128)S(1)} %get-tuple-element.16.came_ty, f32[2,2,256,128]{3,2,1,0:T(8,128)S(1)} %get-tuple-element.17.came_up, ...), custom_call_target="tpu_custom_call" | custom-call | tf_op jit(solution)/shard_map/finish/pallas_call | solution.py:424
Async XLA Ops:
  0.6 16.5 %copy-start = (bf16[2,4,256,256]{3,2,1,0:T(8,128)(2,1)S(1)}, bf16[2,4,256,256]{3,2,1,0:T(8,128)(2,1)}, u32[]{:S(2)}) copy-start(bf16[2,4,256,256]{3,2,1,0:T(8,128)(2,1)} %constant.2.clone.tables) | copy-start | bytes 3145732
  0.6 16.5 %copy-start.4 = (s32[1,2]{1,0:T(1,128)S(1)}, s32[1,2]{1,0:T(1,128)}, u32[]{:S(2)}) copy-start(s32[1,2]{1,0:T(1,128)} %counts.1) | copy-start | bytes 28
  0.7 16.5 %copy-start.3 = (s32[1,2,12,2]{2,3,1,0:T(2,128)S(1)}, s32[1,2,12,2]{2,3,1,0:T(2,128)}, u32[]{:S(2)}) copy-start(s32[1,2,12,2]{2,3,1,0:T(2,128)} %param.13) | copy-start | bytes 580
  0.7 16.5 %copy-start.2 = (f32[256,256]{1,0:T(8,128)S(1)}, f32[256,256]{1,0:T(8,128)}, u32[]{:S(2)}) copy-start(f32[256,256]{1,0:T(8,128)} %probe_im.1) | copy-start | bytes 786436
  0.7 16.5 %copy-start.1 = (f32[256,256]{1,0:T(8,128)S(1)}, f32[256,256]{1,0:T(8,128)}, u32[]{:S(2)}) copy-start(f32[256,256]{1,0:T(8,128)} %probe_re.1) | copy-start | bytes 786436

commit v4 on v3

--- a/solution.py
+++ b/solution.py
@@ -16,6 +16,8 @@
 NTX = 128
 ROWS = TR + N
 MESH = pl.DeviceIdType.MESH
+EDGE = NTX // 2
+DETOUR = ((1, 0, 0), (2, 0, 1), (3, 1, 0), (3, 1, 1))
 F32 = jnp.float32
 BF16 = jnp.bfloat16
 
@@ -46,6 +48,7 @@
 def halo_kernel(
     obj_re, obj_im, amp, reg, amp_out, raw, perm,
     ty_send, ty_recv, up_send, up_recv, diag_send, diag_recv, own_sem, raw_sem,
+    relay, detour_send, detour_recv, relay_send,
 ):
     tx, ty = lax.axis_index("tx"), lax.axis_index("ty")
     up, down = lax.rem(tx + NTX - 1, NTX), lax.rem(tx + 1, NTX)
@@ -53,6 +56,18 @@
     barrier = pltpu.get_barrier_semaphore()
     for device in (partner, (up, ty), (down, ty)):
         pl.semaphore_signal(barrier, inc=1, device_id=device, device_id_type=MESH)
+    is_relay = (tx > EDGE) & (tx <= EDGE + 6) & (lax.rem(tx, 2) == 0)
+
+    @pl.when((tx == EDGE) | (tx == EDGE - 1))
+    def _():
+        for k in range(1, 4):
+            pl.semaphore_signal(barrier, inc=1, device_id=(EDGE + 2 * k, ty), device_id_type=MESH)
+
+    @pl.when(is_relay)
+    def _():
+        for device in (EDGE, EDGE - 1):
+            pl.semaphore_signal(barrier, inc=1, device_id=(device, ty), device_id_type=MESH)
+
     raw_copies = []
     for t in range(2):
         c = pltpu.make_async_copy(amp.at[0, 0, :, :, pl.ds(t * H, H)], raw.at[t], raw_sem.at[t])
@@ -67,7 +82,20 @@
             own.append(c)
     i, j = (lax.broadcasted_iota(jnp.int32, (N, N), d) for d in range(2))
     perm[...] = jnp.where(i == jnp.where(j < H, 2 * j, 2 * (j - H) + 1), 1.0, 0.0).astype(BF16)
-    pl.semaphore_wait(barrier, 3)
+    at_edge = (tx == EDGE) | (tx == EDGE - 1)
+
+    @pl.when(at_edge)
+    def _():
+        pl.semaphore_wait(barrier, 6)
+
+    @pl.when(is_relay)
+    def _():
+        pl.semaphore_wait(barrier, 5)
+
+    @pl.when(jnp.logical_not(at_edge | is_relay))
+    def _():
+        pl.semaphore_wait(barrier, 3)
+
 
     edge = pl.multiple_of((1 - ty) * H, H)
     across = [[], []]
@@ -80,15 +108,55 @@
                 device_id=partner, device_id_type=MESH)
             c.start()
             across[half].append(c)
-    below = []
-    for p, obj in enumerate((obj_re, obj_im)):
-        for t in range(2):
-            c = pltpu.make_async_remote_copy(
-                src_ref=obj.at[pl.ds(0, N), pl.ds(t * H, H)], dst_ref=reg.at[p, ty + t, pl.ds(TR, N)],
-                send_sem=up_send.at[p, t], recv_sem=up_recv.at[p, t],
-                device_id=(up, ty), device_id_type=MESH)
-            c.start()
-            below.append(c)
+    objs = (obj_re, obj_im)
+    blocks = [(p, t) for p in range(2) for t in range(2)]
+
+    def below(p, t):
+        return pltpu.make_async_remote_copy(
+            src_ref=objs[p].at[pl.ds(0, N), pl.ds(t * H, H)], dst_ref=reg.at[p, ty + t, pl.ds(TR, N)],
+            send_sem=up_send.at[p, t], recv_sem=up_recv.at[p, t],
+            device_id=(up, ty), device_id_type=MESH)
+
+    def detour(n):
+        k, p, t = DETOUR[n]
+        return pltpu.make_async_remote_copy(
+            src_ref=objs[p].at[pl.ds(0, N), pl.ds(t * H, H)], dst_ref=relay.at[max(n - 2, 0)],
+            send_sem=detour_send.at[n], recv_sem=detour_recv.at[max(n - 2, 0)],
+            device_id=(EDGE + 2 * k, ty), device_id_type=MESH)
+
+    def onward(n):
+        _, p, t = DETOUR[n]
+        return pltpu.make_async_remote_copy(
+            src_ref=relay.at[max(n - 2, 0)], dst_ref=reg.at[p, ty + t, pl.ds(TR, N)],
+            send_sem=relay_send.at[max(n - 2, 0)], recv_sem=up_recv.at[p, t],
+            device_id=(EDGE - 1, ty), device_id_type=MESH)
+
+    def diag(p):
+        side = 2 - 2 * ty
+        return pltpu.make_async_remote_copy(
+            src_ref=reg.at[p, side, pl.ds(0, N)], dst_ref=reg.at[p, side, pl.ds(TR, N)],
+            send_sem=diag_send.at[p], recv_sem=diag_recv.at[p],
+            device_id=(up, ty), device_id_type=MESH)
+
+    sends_up = (tx > 0) & (tx != EDGE)
+
+    @pl.when(sends_up)
+    def _():
+        for p, t in blocks:
+            below(p, t).start()
+
+    @pl.when(tx == EDGE)
+    def _():
+        for n in range(4):
+            detour(n).start()
+
+    for n in range(4):
+
+        @pl.when(tx == EDGE + 2 * DETOUR[n][0])
+        def _():
+            detour(n).wait_recv()
+            onward(n).start()
+
     for c in raw_copies:
         c.wait()
 
@@ -100,20 +168,45 @@
         return carry
 
     lax.fori_loop(0, SLOTS // 2, sort_slot, 0)
-    diag = []
     for p in range(2):
         across[0][p].wait()
-        side = 2 - 2 * ty
-        c = pltpu.make_async_remote_copy(
-            src_ref=reg.at[p, side, pl.ds(0, N)], dst_ref=reg.at[p, side, pl.ds(TR, N)],
-            send_sem=diag_send.at[p], recv_sem=diag_recv.at[p],
-            device_id=(up, ty), device_id_type=MESH)
-        c.start()
-        diag.append(c)
+
+        @pl.when(tx > 0)
+        def _():
+            diag(p).start()
+
     lax.fori_loop(SLOTS // 2, SLOTS, sort_slot, 0)
 
-    for c in own + across[1] + below + diag:
+    for c in own + across[1]:
         c.wait()
+
+    @pl.when(sends_up)
+    def _():
+        for p, t in blocks:
+            below(p, t).wait_send()
+
+    @pl.when(tx == EDGE)
+    def _():
+        for n in range(4):
+            detour(n).wait_send()
+
+    for n in range(4):
+
+        @pl.when(tx == EDGE + 2 * DETOUR[n][0])
+        def _():
+            onward(n).wait_send()
+
+    @pl.when(tx > 0)
+    def _():
+        for p in range(2):
+            diag(p).wait_send()
+
+    @pl.when(tx < NTX - 1)
+    def _():
+        for p, t in blocks:
+            below(p, t).wait_recv()
+        for p in range(2):
+            diag(p).wait_recv()
 
 
 def halo(obj_re, obj_im, amp):
@@ -132,6 +225,7 @@
             pltpu.VMEM((N, N), BF16),
             dma((2, 2)), dma((2, 2)), dma((2, 2)), dma((2, 2)), dma((2,)), dma((2,)),
             dma((2, 2)), dma((2,)),
+            pltpu.VMEM((2, N, H), F32), dma((4,)), dma((2,)), dma((2,)),
         ],
         compiler_params=pltpu.CompilerParams(
             collective_id=0, has_side_effects=True, vmem_limit_bytes=20 << 20),
@@ -316,16 +410,19 @@
     yz_mates = [at(core, i, z_high * 4 + j, x) for i, j in yz_at]
     hops = [(1, 2), (1, 1), (1, 3), (1, 0), (0, 2), (0, 1), (0, 3)]
     far_mates = [at(core, y, lax.rem(z_high + i, 2) * 4 + z_low, lax.rem(x + j, 4)) for i, j in hops]
-    greeted = [partner, (up, ty), (down, ty), core_mate] + yz_mates + far_mates
+    greeted = far_mates + yz_mates + [partner, (up, ty), (down, ty), core_mate]
     barrier = pltpu.get_barrier_semaphore()
     for device in greeted:
         pl.semaphore_signal(barrier, inc=1, device_id=device, device_id_type=MESH)
     pl.semaphore_wait(barrier, len(greeted))
 
-    def send(src, dst, send_sem, recv_sem, device):
-        c = pltpu.make_async_remote_copy(
+    def make(src, dst, send_sem, recv_sem, device):
+        return pltpu.make_async_remote_copy(
             src_ref=src, dst_ref=dst, send_sem=send_sem, recv_sem=recv_sem,
             device_id=device, device_id_type=MESH)
+
+    def send(*args):
+        c = make(*args)
         c.start()
         return c
 
@@ -334,7 +431,18 @@
 
     side = 2 - 2 * ty
     core_copy = send(pgrad.at[1 - core], core_in, core_send.at[0], core_recv.at[0], core_mate)
-    diag = send(grad.at[:, side, pl.ds(TR, N)], came_diag, diag_send, diag_recv, (down, ty))
+    diag = make(grad.at[:, side, pl.ds(TR, N)], came_diag, diag_send, diag_recv, (down, ty))
+    below = make(grad.at[:, pl.ds(ty, 2), pl.ds(TR, N)], out_up, up_send, up_recv, (down, ty))
+
+    @pl.when(tx < NTX - 1)
+    def _():
+        diag.start()
+
+    @pl.when(tx == 0)
+    def _():
+        came_diag[...] = jnp.zeros_like(came_diag)
+        out_up[...] = jnp.zeros_like(out_up)
+
     far_rows = send(
         grad.at[:, side, pl.ds(N, N)], out_ty.at[:, pl.ds(N, N)], ty_send.at[1], ty_recv.at[1], partner)
     core_copy.wait()
@@ -343,7 +451,11 @@
     yz_copies = [
         send(acc.at[part(*yz_at[d])], yz_in.at[d], yz_send.at[0, d], yz_recv.at[0, d], yz_mates[d])
         for d in range(15)]
-    diag.wait()
+
+    @pl.when(tx > 0)
+    def _():
+        diag.wait_recv()
+
     for p in range(2):
         edge[p] = grad[p, side, pl.ds(0, N)] + came_diag[p]
     for c in yz_copies:
@@ -355,7 +467,11 @@
     shared[mine] = total
     far_copies = [
         send(shared.at[mine], shared.at[mine], far_send.at[d], far_recv.at[d], far_mates[d]) for d in range(7)]
-    below = send(grad.at[:, pl.ds(ty, 2), pl.ds(TR, N)], out_up, up_send, up_recv, (down, ty))
+
+    @pl.when(tx < NTX - 1)
+    def _():
+        below.start()
+
     for c in far_copies:
         c.wait()
     total = shared[0]
@@ -370,7 +486,16 @@
     for c in yz_copies:
         c.wait()
     core_copy = send(out_full, out_other, core_send.at[1], core_recv.at[1], core_mate)
-    below.wait()
+
+    @pl.when(tx < NTX - 1)
+    def _():
+        diag.wait_send()
+        below.wait_send()
+
+    @pl.when(tx > 0)
+    def _():
+        below.wait_recv()
+
     far_rows.wait()
     near_rows.wait()
     core_copy.wait()

time: 78.7 us -> 72.8 us (0.925)
  Pallas kernels: 77.8 us -> 71.9 us
    pallas_call x1, Pallas kernels: 45.9 us -> 37.1 us  [gather_out(): pl.pallas_call(out_kernel, out_shape=(jax.ShapeDtypeStruct((2, TR, H), F3...]
    pallas_call x1, Pallas kernels: 14.2 us -> 16.9 us  [positions(): pl.pallas_call(positions_kernel, out_shape=(pltpu.VMEM((2, 3, ROWS, H), F...]
where the time goes in v4:
time: 72.8 us; the launch traced here: 72.7 us
  Pallas kernels  71.9 us (99%)
  between operations  0.74 us (1%)
    pallas_call x1, Pallas kernels, gather_out(): pl.pallas_call(out_kernel, out_shape=(jax.ShapeDtypeStruct((2, TR, H), F3...  37.1 us
    pallas_call x1, Pallas kernels, positions(): pl.pallas_call(positions_kernel, out_shape=(pltpu.VMEM((2, 3, ROWS, H), F...  16.9 us
    pallas_call x1, Pallas kernels, halo(): pl.pallas_call(halo_kernel, out_shape=(pltpu.VMEM((2, 3, ROWS, H), F32),...  16.5 us

profile of v4, /device:TPU:1, one launch (start us, length us, event | category | flops | bytes accessed | tf_op | source)
XLA Modules:
  0.0 72.7 jit_solution(17319891420320627417)
XLA Ops:
  0.6 0.0 copy-start
  0.6 0.0 copy-start.4
  0.7 0.0 copy-start.3
  0.7 0.0 copy-start.2
  0.7 0.0 copy-start.1
  0.7 16.5 %halo.1 = (f32[2,3,768,128]{3,2,1,0:T(8,128)S(1)}, f32[12,256,256]{2,1,0:T(8,128)S(1)}) custom-call(f32[512,256]{1,0:T(8,128)} %obj_re.1, f32[512,256]{1,0:T(8,128)} %obj_im.1, f32[1,1,12,256,256]{4,3,2,1,0:T(8,128)} %amp.1), custom_call_target="tpu_custom_call" | custom-call | tf_op jit(solution)/shard_map/halo/pallas_call | solution.py:215
  17.2 0.0 copy-done
  17.3 0.0 copy-done.4
  17.3 0.0 copy-done.3
  17.3 0.0 copy-done.2
  17.3 0.0 copy-done.1
  17.3 16.9 %positions.1 = (f32[2,3,768,128]{3,2,1,0:T(8,128)S(1)}, f32[2,2,256,128]{3,2,1,0:T(8,128)S(1)}) custom-call(s32[1,2,2,12]{3,2,1,0:T(2,128)S(1)} %bitcast.1, s32[1,2]{1,0:T(1,128)S(1)} %copy-done.4, f32[2,3,768,128]{3,2,1,0:T(8,128)S(1)} %get-tuple-element.12.reg, f32[256,256]{1,0:T(8,128)S(1)} %copy-done.1, f32[256,256]{1,0:T(8,128)S(1)} %copy-done.2, ...), custom_call_target="tpu_custom_call" | custom-call | tf_op jit(solution)/shard_map/positions/pallas_call | solution.py:372
  34.2 37.1 %gather_out.1 = (f32[2,512,128]{2,1,0:T(8,128)S(1)}, f32[2,2,256,128]{3,2,1,0:T(8,128)S(1)}, f32[512,128]{1,0:T(8,128)S(1)}, f32[512,128]{1,0:T(8,128)S(1)}) custom-call(f32[2,3,768,128]{3,2,1,0:T(8,128)S(1)} %get-tuple-element.14.grad, f32[2,2,256,128]{3,2,1,0:T(8,128)S(1)} %get-tuple-element.15.pgrad), custom_call_target="tpu_custom_call" | custom-call | tf_op jit(solution)/shard_map/gather_out/pallas_call | solution.py:525
  71.3 1.3 %finish.1 = (f32[512,256]{1,0:T(8,128)}, f32[512,256]{1,0:T(8,128)}, f32[256,256]{1,0:T(8,128)}, f32[256,256]{1,0:T(8,128)}) custom-call(f32[2,3,768,128]{3,2,1,0:T(8,128)S(1)} %get-tuple-element.14.grad, f32[2,512,128]{2,1,0:T(8,128)S(1)} %get-tuple-element.16.came_ty, f32[2,2,256,128]{3,2,1,0:T(8,128)S(1)} %get-tuple-element.17.came_up, ...), custom_call_target="tpu_custom_call" | custom-call | tf_op jit(solution)/shard_map/finish/pallas_call | solution.py:549
Async XLA Ops:
  0.6 16.6 %copy-start = (bf16[2,4,256,256]{3,2,1,0:T(8,128)(2,1)S(1)}, bf16[2,4,256,256]{3,2,1,0:T(8,128)(2,1)}, u32[]{:S(2)}) copy-start(bf16[2,4,256,256]{3,2,1,0:T(8,128)(2,1)} %constant.2.clone.tables) | copy-start | bytes 3145732
  0.6 16.6 %copy-start.4 = (s32[1,2]{1,0:T(1,128)S(1)}, s32[1,2]{1,0:T(1,128)}, u32[]{:S(2)}) copy-start(s32[1,2]{1,0:T(1,128)} %counts.1) | copy-start | bytes 28
  0.7 16.6 %copy-start.3 = (s32[1,2,12,2]{2,3,1,0:T(2,128)S(1)}, s32[1,2,12,2]{2,3,1,0:T(2,128)}, u32[]{:S(2)}) copy-start(s32[1,2,12,2]{2,3,1,0:T(2,128)} %param.13) | copy-start | bytes 580
  0.7 16.6 %copy-start.2 = (f32[256,256]{1,0:T(8,128)S(1)}, f32[256,256]{1,0:T(8,128)}, u32[]{:S(2)}) copy-start(f32[256,256]{1,0:T(8,128)} %probe_im.1) | copy-start | bytes 786436
  0.7 16.6 %copy-start.1 = (f32[256,256]{1,0:T(8,128)S(1)}, f32[256,256]{1,0:T(8,128)}, u32[]{:S(2)}) copy-start(f32[256,256]{1,0:T(8,128)} %probe_re.1) | copy-start | bytes 786436

commit v5 on v4

--- a/solution.py
+++ b/solution.py
@@ -16,6 +16,9 @@
 NTX = 128
 ROWS = TR + N
 MESH = pl.DeviceIdType.MESH
+CH = 32
+LAST = 4
+PIECE = TR // 8
 EDGE = NTX // 2
 DETOUR = ((1, 0, 0), (2, 0, 1), (3, 1, 0), (3, 1, 1))
 F32 = jnp.float32
@@ -233,16 +236,7 @@
     )(*(pltpu.with_memory_space_constraint(x, pltpu.HBM) for x in (obj_re, obj_im, amp)))
 
 
-def positions_kernel(
-    offsets, counts, reg, probe_re, probe_im, tables, amp, grad, pgrad, win, sp, mid,
-):
-    tx, ty = lax.axis_index("tx"), lax.axis_index("ty")
-    live = counts[0, ty]
-    probe = (probe_re, probe_im)
-    CH = 32
-
-    grad[...] = jnp.zeros_like(grad)
-    pgrad[...] = jnp.zeros_like(pgrad)
+def pair_of_positions(reg, probe_re, probe_im, tables, amp, win, sp, mid):
     lane = lax.broadcasted_iota(jnp.int32, (CH, H), 1)
 
     def put(s, q, rows, lanes, value):
@@ -314,7 +308,7 @@
                     put(s, q, pl.ds(j * CH, CH), lanes(p), a + b)
                     put(s, q, pl.ds(H + j * CH, CH), lanes(p), a - b)
 
-    def leave(s, place):
+    def leave(s, place, add_rows, add_probe):
         row_at, col_at = place
         ahead = lax.rem(col_at, H)
         to_next = lane < col_at
@@ -330,22 +324,15 @@
                 wr, wi = win[s, 0, t, rows, :], win[s, 1, t, rows, :]
                 g[0][t] = pltpu.roll(pr * chi[0] + pi * chi[1], ahead, 1)
                 g[1][t] = pltpu.roll(pr * chi[1] - pi * chi[0], ahead, 1)
-                pgrad[0, t, rows, :] += wr * chi[0] + wi * chi[1]
-                pgrad[1, t, rows, :] += wr * chi[1] - wi * chi[0]
-            at = pl.ds(row_at + j * CH, CH)
+                add_probe(t, rows, wr * chi[0] + wi * chi[1], wr * chi[1] - wi * chi[0])
             for p in range(2):
-                grad[p, 0, at, :] += jnp.where(to_next, 0.0, g[p][0])
-                grad[p, 1, at, :] += jnp.where(to_next, g[p][0], g[p][1])
-                grad[p, 2, at, :] += jnp.where(to_next, g[p][1], 0.0)
-
-    def place_of(i):
-        return offsets[0, ty, 0, i] - tx * TR, offsets[0, ty, 1, i] - ty * H
-
-    def pair(k, carry):
-        ids = [2 * k, jnp.minimum(2 * k + 1, live - 1)]
-        used = [True, 2 * k + 1 < live]
-        places = [place_of(i) for i in ids]
-        steps = [
+                add_rows(s, row_at, j, p, (
+                    jnp.where(to_next, 0.0, g[p][0]),
+                    jnp.where(to_next, g[p][0], g[p][1]),
+                    jnp.where(to_next, g[p][1], 0.0)))
+
+    def pair(places, ids, used, add_rows, add_probe):
+        stages = [
             lambda s: enter(s, places[s]),
             lambda s: [right(s, q, q) for q in range(2)],
             lambda s: fold_rows(s),
@@ -354,16 +341,46 @@
             lambda s: [left(s, h, h) for h in range(2)],
             lambda s: unfold_rows(s),
             lambda s: [right(s, q, 2 + q) for q in range(2)],
-            lambda s: leave(s, places[s]),
+            lambda s: leave(s, places[s], add_rows, add_probe),
         ]
-        steps[0](0)
-        for n in range(1, len(steps)):
-            steps[n](0)
-            steps[n - 1](1)
-        steps[-1](1)
+        stages[0](0)
+        for n in range(1, len(stages)):
+            stages[n](0)
+            stages[n - 1](1)
+        stages[-1](1)
+
+    return pair
+
+
+def place_of(offsets, tx, ty, i):
+    row_at, col_at = offsets[0, ty, 0, i] - tx * TR, offsets[0, ty, 1, i] - ty * H
+    return jnp.clip(row_at, 0, TR - 1), jnp.clip(col_at, 0, H)
+
+
+def positions_kernel(
+    offsets, counts, reg, probe_re, probe_im, tables, amp, grad, pgrad, win, sp, mid,
+):
+    tx, ty = lax.axis_index("tx"), lax.axis_index("ty")
+    here = jnp.maximum(counts[0, ty] - LAST, 0)
+    grad[...] = jnp.zeros_like(grad)
+    pgrad[...] = jnp.zeros_like(pgrad)
+    pair = pair_of_positions(reg, probe_re, probe_im, tables, amp, win, sp, mid)
+
+    def add_rows(s, row_at, j, p, tiles):
+        at = pl.ds(row_at + j * CH, CH)
+        for t in range(3):
+            grad[p, t, at, :] += tiles[t]
+
+    def add_probe(t, rows, re, im):
+        pgrad[0, t, rows, :] += re
+        pgrad[1, t, rows, :] += im
+
+    def step(k, carry):
+        ids = [2 * k, jnp.minimum(2 * k + 1, here - 1)]
+        pair([place_of(offsets, tx, ty, i) for i in ids], ids, [True, 2 * k + 1 < here], add_rows, add_probe)
         return carry
 
-    lax.fori_loop(0, (live + 1) // 2, pair, 0)
+    lax.fori_loop(0, (here + 1) // 2, step, 0)
 
 
 def positions(offsets, counts, reg, probe_re, probe_im, tables, amp):
@@ -388,10 +405,10 @@
 
 
 def out_kernel(
-    grad, pgrad, out_ty, out_up, out_full, out_other,
-    came_diag, edge, core_in, acc, yz_in, shared,
+    offsets, counts, reg, probe_re, probe_im, tables, amp, grad_in, pgrad_in, grad, out_ty, out_up, out_full, out_other,
+    pgrad, placed, win, sp, mid, came_diag, edge, core_in, acc, xy_in, shared,
     ty_send, ty_recv, up_send, up_recv, diag_send, diag_recv,
-    core_send, core_recv, yz_send, yz_recv, far_send, far_recv,
+    core_send, core_recv, xy_send, xy_recv, z_send, z_recv,
 ):
     tx, ty = lax.axis_index("tx"), lax.axis_index("ty")
     up, down = lax.rem(tx + NTX - 1, NTX), lax.rem(tx + 1, NTX)
@@ -403,17 +420,41 @@
         return (((lax.rem(x_, 2) * 8 + z_) * 4 + y_) * 2 + core_, x_ // 2)
 
     core_mate = at(1 - core, y, z, x)
-    z_low, z_high = lax.rem(z, 4), z // 4
     steps = [(i, j) for i in range(4) for j in range(4) if i or j]
     steps.sort(key=lambda s: -(min(s[0], 4 - s[0]) + min(s[1], 4 - s[1])))
-    yz_at = [(lax.rem(y + i, 4), lax.rem(z_low + j, 4)) for i, j in steps]
-    yz_mates = [at(core, i, z_high * 4 + j, x) for i, j in yz_at]
-    hops = [(1, 2), (1, 1), (1, 3), (1, 0), (0, 2), (0, 1), (0, 3)]
-    far_mates = [at(core, y, lax.rem(z_high + i, 2) * 4 + z_low, lax.rem(x + j, 4)) for i, j in hops]
-    greeted = far_mates + yz_mates + [partner, (up, ty), (down, ty), core_mate]
+    xy_at = [(lax.rem(y + i, 4), lax.rem(x + j, 4)) for i, j in steps]
+    xy_mates = [at(core, i, z, j) for i, j in xy_at]
+    z_mates = [at(core, y, lax.rem(z + d, 8), x) for d in (4, 3, 5, 2, 6, 1, 7)]
+    greeted = z_mates + xy_mates + [partner, (up, ty), (down, ty), core_mate]
     barrier = pltpu.get_barrier_semaphore()
     for device in greeted:
         pl.semaphore_signal(barrier, inc=1, device_id=device, device_id_type=MESH)
+
+    live = counts[0, ty]
+    for margin in (0, CH + N):
+        placed[:, :, :, pl.ds(margin, CH), :] = jnp.zeros((LAST, 2, 3, CH, H), F32)
+    pgrad[...] = pgrad_in[...]
+    pair = pair_of_positions(reg, probe_re, probe_im, tables, amp, win, sp, mid)
+
+    def add_probe(t, rows, re, im):
+        pgrad[0, t, rows, :] += re
+        pgrad[1, t, rows, :] += im
+
+    def id_of(n):
+        return jnp.maximum(live - LAST + n, 0)
+
+    def step(k, carry):
+        ids = [id_of(2 * k + s) for s in range(2)]
+
+        def add_rows(s, row_at, j, p, tiles):
+            for t in range(3):
+                placed[2 * k + s, p, t, pl.ds(CH + j * CH, CH), :] = tiles[t]
+
+        pair([place_of(offsets, tx, ty, i) for i in ids], ids,
+             [live - LAST + 2 * k + s >= 0 for s in range(2)], add_rows, add_probe)
+        return carry
+
+    lax.fori_loop(0, LAST // 2, step, 0)
     pl.semaphore_wait(barrier, len(greeted))
 
     def make(src, dst, send_sem, recv_sem, device):
@@ -431,6 +472,21 @@
 
     side = 2 - 2 * ty
     core_copy = send(pgrad.at[1 - core], core_in, core_send.at[0], core_recv.at[0], core_mate)
+
+    firsts = [place_of(offsets, tx, ty, id_of(n))[0] for n in range(LAST)]
+
+    def place_rows(j, carry):
+        rows = pl.ds(pl.multiple_of(j * CH, CH), CH)
+        for p in range(2):
+            for t in range(3):
+                total = grad_in[p, t, rows, :]
+                for n in range(LAST):
+                    at = jnp.clip(j * CH - firsts[n] + CH, 0, CH + N)
+                    total = total + placed[n, p, t, pl.ds(at, CH), :]
+                grad[p, t, rows, :] = total
+        return carry
+
+    lax.fori_loop(0, ROWS // CH, place_rows, 0)
     diag = make(grad.at[:, side, pl.ds(TR, N)], came_diag, diag_send, diag_recv, (down, ty))
     below = make(grad.at[:, pl.ds(ty, 2), pl.ds(TR, N)], out_up, up_send, up_recv, (down, ty))
 
@@ -443,49 +499,61 @@
         came_diag[...] = jnp.zeros_like(came_diag)
         out_up[...] = jnp.zeros_like(out_up)
 
-    far_rows = send(
-        grad.at[:, side, pl.ds(N, N)], out_ty.at[:, pl.ds(N, N)], ty_send.at[1], ty_recv.at[1], partner)
+    pieces = []
+
+    def send_pieces(count):
+        for _ in range(count):
+            n = (len(pieces) + 4) % 8
+            rows = pl.ds(n * PIECE, PIECE)
+            src = grad.at[:, side, rows] if n >= 4 else edge.at[:, rows]
+            pieces.append(send(src, out_ty.at[:, rows], ty_send.at[n], ty_recv.at[n], partner))
+
+    def start_below():
+        @pl.when(tx < NTX - 1)
+        def _():
+            below.start()
+
+    def add_edge():
+        @pl.when(tx > 0)
+        def _():
+            diag.wait_recv()
+
+        for p in range(2):
+            edge[p] = grad[p, side, pl.ds(0, N)] + came_diag[p]
+
+    send_pieces(2)
     core_copy.wait()
     for t in range(2):
         acc[pl.ds(t * N, N), :] = pgrad[core, t] + core_in[t]
-    yz_copies = [
-        send(acc.at[part(*yz_at[d])], yz_in.at[d], yz_send.at[0, d], yz_recv.at[0, d], yz_mates[d])
+    xy_copies = [
+        send(acc.at[part(*xy_at[d])], xy_in.at[d], xy_send.at[0, d], xy_recv.at[0, d], xy_mates[d])
         for d in range(15)]
-
-    @pl.when(tx > 0)
-    def _():
-        diag.wait_recv()
-
-    for p in range(2):
-        edge[p] = grad[p, side, pl.ds(0, N)] + came_diag[p]
-    for c in yz_copies:
+    send_pieces(2)
+    add_edge()
+    for c in xy_copies:
         c.wait()
-    total = acc[part(y, z_low), :]
+    total = acc[part(y, x), :]
     for d in range(15):
-        total = total + yz_in[d]
-    mine = x * 2 + z_high
-    shared[mine] = total
-    far_copies = [
-        send(shared.at[mine], shared.at[mine], far_send.at[d], far_recv.at[d], far_mates[d]) for d in range(7)]
-
-    @pl.when(tx < NTX - 1)
-    def _():
-        below.start()
-
-    for c in far_copies:
+        total = total + xy_in[d]
+    shared[z] = total
+    z_copies = [
+        send(shared.at[z], shared.at[z], z_send.at[d], z_recv.at[d], z_mates[d]) for d in range(7)]
+    start_below()
+    send_pieces(4)
+    for c in z_copies:
         c.wait()
     total = shared[0]
     for d in range(1, 8):
         total = total + shared[d]
-    out_full[part(y, z_low), :] = total * (1.0 / (NTX * 2 * SLOTS))
-    yz_copies = [
-        send(out_full.at[part(y, z_low)], out_full.at[part(y, z_low)],
-             yz_send.at[1, d], yz_recv.at[1, d], yz_mates[d])
+    out_full[part(y, x), :] = total * (1.0 / (NTX * 2 * SLOTS))
+    xy_copies = [
+        send(out_full.at[part(y, x)], out_full.at[part(y, x)], xy_send.at[1, d], xy_recv.at[1, d], xy_mates[d])
         for d in range(15)]
-    near_rows = send(edge, out_ty.at[:, pl.ds(0, N)], ty_send.at[0], ty_recv.at[0], partner)
-    for c in yz_copies:
+    for c in xy_copies:
         c.wait()
     core_copy = send(out_full, out_other, core_send.at[1], core_recv.at[1], core_mate)
+    for c in pieces:
+        c.wait()
 
     @pl.when(tx < NTX - 1)
     def _():
@@ -496,8 +564,6 @@
     def _():
         below.wait_recv()
 
-    far_rows.wait()
-    near_rows.wait()
     core_copy.wait()
 
 
@@ -517,35 +583,42 @@
         pout_im[:, lanes] = jnp.where(core == 0, b, a)
 
 
-def gather_out(grad, pgrad):
+def gather_out(offsets, counts, reg, probe_re, probe_im, tables, amp, grad, pgrad):
     vmem = pl.BlockSpec(memory_space=pltpu.VMEM)
     dma = pltpu.SemaphoreType.DMA
     tile = jax.ShapeDtypeStruct((TR, N), F32)
     patch = jax.ShapeDtypeStruct((N, N), F32)
-    came = pl.pallas_call(
+    smem = pl.BlockSpec(memory_space=pltpu.SMEM)
+    grad, *came = pl.pallas_call(
         out_kernel,
         out_shape=(
+            pltpu.VMEM((2, 3, ROWS, H), F32),
             jax.ShapeDtypeStruct((2, TR, H), F32),
             jax.ShapeDtypeStruct((2, 2, N, H), F32),
             jax.ShapeDtypeStruct((2 * N, H), F32),
             jax.ShapeDtypeStruct((2 * N, H), F32),
         ),
-        in_specs=[vmem, vmem],
-        out_specs=(vmem, vmem, vmem, vmem),
+        in_specs=[smem, smem] + [vmem] * 7,
+        out_specs=(vmem,) * 5,
         scratch_shapes=[
+            pltpu.VMEM((2, 2, N, H), F32),
+            pltpu.VMEM((LAST, 2, 3, N + 2 * CH, H), F32),
+            pltpu.VMEM((2, 2, 2, N, H), F32),
+            pltpu.VMEM((2, 2, 2, N, N), BF16),
+            pltpu.VMEM((2, 2, N, N), F32),
             pltpu.VMEM((2, N, H), F32),
             pltpu.VMEM((2, N, H), F32),
             pltpu.VMEM((2, N, H), F32),
             pltpu.VMEM((2 * N, H), F32),
             pltpu.VMEM((15, 32, H), F32),
             pltpu.VMEM((8, 32, H), F32),
-            dma((2,)), dma((2,)), dma(()), dma(()), dma(()), dma(()),
+            dma((8,)), dma((8,)), dma(()), dma(()), dma(()), dma(()),
             dma((2,)), dma((2,)), dma((2, 15)), dma((2, 15)), dma((7,)), dma((7,)),
         ],
         compiler_params=pltpu.CompilerParams(
             collective_id=1, has_side_effects=True, vmem_limit_bytes=20 << 20),
         name="gather_out",
-    )(grad, pgrad)
+    )(offsets, counts, reg, probe_re, probe_im, tables, amp, grad, pgrad)
     return pl.pallas_call(
         finish_kernel,
         out_shape=(tile, tile, patch, patch),
@@ -559,8 +632,9 @@
 def per_device(obj_re, obj_im, probe_re, probe_im, amplitude, offsets, counts):
     tables = jnp.asarray(half_dft_tables())
     reg, amp = halo(obj_re, obj_im, amplitude)
-    grad, pgrad = positions(jnp.swapaxes(offsets, 2, 3), counts, reg, probe_re, probe_im, tables, amp)
-    return gather_out(grad, pgrad)
+    shared = (jnp.swapaxes(offsets, 2, 3), counts, reg, probe_re, probe_im, tables, amp)
+    grad, pgrad = positions(*shared)
+    return gather_out(*shared, grad, pgrad)
 
 
 def solution(mesh):

time: 72.8 us -> 71.5 us (0.982)
  Pallas kernels: 71.9 us -> 70.6 us
    pallas_call x1, Pallas kernels: 16.9 us -> 0.76 us  [positions(): pl.pallas_call(positions_kernel, out_shape=(pltpu.VMEM((2, 3, ROWS, H), F...]
    pallas_call x1, Pallas kernels: 37.1 us -> 52 us  [gather_out(): pl.pallas_call(out_kernel, out_shape=(pltpu.VMEM((2, 3, ROWS, H), F32), j...]
where the time goes in v5:
time: 71.5 us; the launch traced here: 71.4 us
  Pallas kernels  70.6 us (99%)
  between operations  0.73 us (1%)
    pallas_call x1, Pallas kernels, gather_out(): pl.pallas_call(out_kernel, out_shape=(pltpu.VMEM((2, 3, ROWS, H), F32), j...  52 us
    pallas_call x1, Pallas kernels, halo(): pl.pallas_call(halo_kernel, out_shape=(pltpu.VMEM((2, 3, ROWS, H), F32),...  16.5 us

profile of v5, /device:TPU:1, one launch (start us, length us, event | category | flops | bytes accessed | tf_op | source)
XLA Modules:
  0.0 71.4 jit_solution(337415112684313957)
XLA Ops:
  0.6 0.0 copy-start
  0.6 0.0 copy-start.4
  0.7 0.0 copy-start.2
  0.7 0.0 copy-start.1
  0.7 0.0 copy-start.3
  0.7 16.5 %halo.1 = (f32[2,3,768,128]{3,2,1,0:T(8,128)S(1)}, f32[12,256,256]{2,1,0:T(8,128)S(1)}) custom-call(f32[512,256]{1,0:T(8,128)} %obj_re.1, f32[512,256]{1,0:T(8,128)} %obj_im.1, f32[1,1,12,256,256]{4,3,2,1,0:T(8,128)} %amp.1), custom_call_target="tpu_custom_call" | custom-call | tf_op jit(solution)/shard_map/halo/pallas_call | solution.py:218
  17.2 0.0 copy-done
  17.3 0.0 copy-done.4
  17.3 0.0 copy-done.2
  17.3 0.0 copy-done.1
  17.3 0.0 copy-done.3
  17.3 0.8 %positions.1 = (f32[2,3,768,128]{3,2,1,0:T(8,128)S(1)}, f32[2,2,256,128]{3,2,1,0:T(8,128)S(1)}) custom-call(s32[1,2,2,12]{3,2,1,0:T(2,128)S(1)} %bitcast.1, s32[1,2]{1,0:T(1,128)S(1)} %copy-done.4, f32[2,3,768,128]{3,2,1,0:T(8,128)S(1)} %get-tuple-element.13.reg, f32[256,256]{1,0:T(8,128)S(1)} %copy-done.1, f32[256,256]{1,0:T(8,128)S(1)} %copy-done.2, ...), custom_call_target="tpu_custom_call" | custom-call | tf_op jit(solution)/shard_map/positions/pallas_call | solution.py:389
  18.1 52.0 %gather_out.1 = (f32[2,3,768,128]{3,2,1,0:T(8,128)S(1)}, f32[2,512,128]{2,1,0:T(8,128)S(1)}, f32[2,2,256,128]{3,2,1,0:T(8,128)S(1)}, f32[512,128]{1,0:T(8,128)S(1)}, f32[512,128]{1,0:T(8,128)S(1)}) custom-call(s32[1,2,2,12]{3,2,1,0:T(2,128)S(1)} %bitcast.2, s32[1,2]{1,0:T(1,128)S(1)} %copy-done.4, f32[2,3,768,128]{3,2,1,0:T(8,128)S(1)} %get-tuple-element.13.reg, ...), custom_call_target="tpu_custom_call" | custom-call | tf_op jit(solution)/shard_map/gather_out/pallas_call | solution.py:592
  70.1 1.3 %finish.1 = (f32[512,256]{1,0:T(8,128)}, f32[512,256]{1,0:T(8,128)}, f32[256,256]{1,0:T(8,128)}, f32[256,256]{1,0:T(8,128)}) custom-call(f32[2,3,768,128]{3,2,1,0:T(8,128)S(1)} %get-tuple-element.17.grad, f32[2,512,128]{2,1,0:T(8,128)S(1)} %get-tuple-element.18.came_ty, f32[2,2,256,128]{3,2,1,0:T(8,128)S(1)} %get-tuple-element.19.came_up, ...), custom_call_target="tpu_custom_call" | custom-call | tf_op jit(solution)/shard_map/finish/pallas_call | solution.py:622
Async XLA Ops:
  0.6 16.6 %copy-start = (bf16[2,4,256,256]{3,2,1,0:T(8,128)(2,1)S(1)}, bf16[2,4,256,256]{3,2,1,0:T(8,128)(2,1)}, u32[]{:S(2)}) copy-start(bf16[2,4,256,256]{3,2,1,0:T(8,128)(2,1)} %constant.2.clone.tables) | copy-start | bytes 3145732
  0.6 16.6 %copy-start.4 = (s32[1,2]{1,0:T(1,128)S(1)}, s32[1,2]{1,0:T(1,128)}, u32[]{:S(2)}) copy-start(s32[1,2]{1,0:T(1,128)} %counts.3) | copy-start | bytes 28
  0.7 16.6 %copy-start.2 = (f32[256,256]{1,0:T(8,128)S(1)}, f32[256,256]{1,0:T(8,128)}, u32[]{:S(2)}) copy-start(f32[256,256]{1,0:T(8,128)} %probe_im.3) | copy-start | bytes 786436
  0.7 16.6 %copy-start.1 = (f32[256,256]{1,0:T(8,128)S(1)}, f32[256,256]{1,0:T(8,128)}, u32[]{:S(2)}) copy-start(f32[256,256]{1,0:T(8,128)} %probe_re.3) | copy-start | bytes 786436
  0.7 16.6 %copy-start.3 = (s32[1,2,12,2]{2,3,1,0:T(2,128)S(1)}, s32[1,2,12,2]{2,3,1,0:T(2,128)}, u32[]{:S(2)}) copy-start(s32[1,2,12,2]{2,3,1,0:T(2,128)} %param.13) | copy-start | bytes 580

commit v6 on v5

--- a/solution.py
+++ b/solution.py
@@ -17,7 +17,7 @@
 ROWS = TR + N
 MESH = pl.DeviceIdType.MESH
 CH = 32
-LAST = 4
+LAST = 8
 PIECE = TR // 8
 EDGE = NTX // 2
 DETOUR = ((1, 0, 0), (2, 0, 1), (3, 1, 0), (3, 1, 1))

time: 71.5 us -> 70 us (0.979)
  Pallas kernels: 70.6 us -> 69.2 us
    pallas_call x1, Pallas kernels: 52 us -> 50.5 us  [gather_out(): pl.pallas_call(out_kernel, out_shape=(pltpu.VMEM((2, 3, ROWS, H), F32), j...]
where the time goes in v6:
time: 70 us; the launch traced here: 69.9 us
  Pallas kernels  69.2 us (99%)
  between operations  0.73 us (1%)
    pallas_call x1, Pallas kernels, gather_out(): pl.pallas_call(out_kernel, out_shape=(pltpu.VMEM((2, 3, ROWS, H), F32), j...  50.5 us
    pallas_call x1, Pallas kernels, halo(): pl.pallas_call(halo_kernel, out_shape=(pltpu.VMEM((2, 3, ROWS, H), F32),...  16.5 us

profile of v6, /device:TPU:1, one launch (start us, length us, event | category | flops | bytes accessed | tf_op | source)
XLA Modules:
  0.0 69.9 jit_solution(9032094474437586774)
XLA Ops:
  0.6 0.0 copy-start
  0.6 0.0 copy-start.4
  0.7 0.0 copy-start.2
  0.7 0.0 copy-start.1
  0.7 0.0 copy-start.3
  0.7 16.5 %halo.1 = (f32[2,3,768,128]{3,2,1,0:T(8,128)S(1)}, f32[12,256,256]{2,1,0:T(8,128)S(1)}) custom-call(f32[512,256]{1,0:T(8,128)} %obj_re.1, f32[512,256]{1,0:T(8,128)} %obj_im.1, f32[1,1,12,256,256]{4,3,2,1,0:T(8,128)} %amp.1), custom_call_target="tpu_custom_call" | custom-call | tf_op jit(solution)/shard_map/halo/pallas_call | solution.py:218
  17.2 0.0 copy-done
  17.3 0.0 copy-done.4
  17.3 0.0 copy-done.2
  17.3 0.0 copy-done.1
  17.3 0.0 copy-done.3
  17.3 0.8 %positions.1 = (f32[2,3,768,128]{3,2,1,0:T(8,128)S(1)}, f32[2,2,256,128]{3,2,1,0:T(8,128)S(1)}) custom-call(s32[1,2,2,12]{3,2,1,0:T(2,128)S(1)} %bitcast.1, s32[1,2]{1,0:T(1,128)S(1)} %copy-done.4, f32[2,3,768,128]{3,2,1,0:T(8,128)S(1)} %get-tuple-element.13.reg, f32[256,256]{1,0:T(8,128)S(1)} %copy-done.1, f32[256,256]{1,0:T(8,128)S(1)} %copy-done.2, ...), custom_call_target="tpu_custom_call" | custom-call | tf_op jit(solution)/shard_map/positions/pallas_call | solution.py:389
  18.1 50.5 %gather_out.1 = (f32[2,3,768,128]{3,2,1,0:T(8,128)S(1)}, f32[2,512,128]{2,1,0:T(8,128)S(1)}, f32[2,2,256,128]{3,2,1,0:T(8,128)S(1)}, f32[512,128]{1,0:T(8,128)S(1)}, f32[512,128]{1,0:T(8,128)S(1)}) custom-call(s32[1,2,2,12]{3,2,1,0:T(2,128)S(1)} %bitcast.2, s32[1,2]{1,0:T(1,128)S(1)} %copy-done.4, f32[2,3,768,128]{3,2,1,0:T(8,128)S(1)} %get-tuple-element.13.reg, ...), custom_call_target="tpu_custom_call" | custom-call | tf_op jit(solution)/shard_map/gather_out/pallas_call | solution.py:592
  68.6 1.3 %finish.1 = (f32[512,256]{1,0:T(8,128)}, f32[512,256]{1,0:T(8,128)}, f32[256,256]{1,0:T(8,128)}, f32[256,256]{1,0:T(8,128)}) custom-call(f32[2,3,768,128]{3,2,1,0:T(8,128)S(1)} %get-tuple-element.17.grad, f32[2,512,128]{2,1,0:T(8,128)S(1)} %get-tuple-element.18.came_ty, f32[2,2,256,128]{3,2,1,0:T(8,128)S(1)} %get-tuple-element.19.came_up, ...), custom_call_target="tpu_custom_call" | custom-call | tf_op jit(solution)/shard_map/finish/pallas_call | solution.py:622
Async XLA Ops:
  0.6 16.6 %copy-start = (bf16[2,4,256,256]{3,2,1,0:T(8,128)(2,1)S(1)}, bf16[2,4,256,256]{3,2,1,0:T(8,128)(2,1)}, u32[]{:S(2)}) copy-start(bf16[2,4,256,256]{3,2,1,0:T(8,128)(2,1)} %constant.2.clone.tables) | copy-start | bytes 3145732
  0.6 16.6 %copy-start.4 = (s32[1,2]{1,0:T(1,128)S(1)}, s32[1,2]{1,0:T(1,128)}, u32[]{:S(2)}) copy-start(s32[1,2]{1,0:T(1,128)} %counts.3) | copy-start | bytes 28
  0.7 16.6 %copy-start.2 = (f32[256,256]{1,0:T(8,128)S(1)}, f32[256,256]{1,0:T(8,128)}, u32[]{:S(2)}) copy-start(f32[256,256]{1,0:T(8,128)} %probe_im.3) | copy-start | bytes 786436
  0.7 16.6 %copy-start.1 = (f32[256,256]{1,0:T(8,128)S(1)}, f32[256,256]{1,0:T(8,128)}, u32[]{:S(2)}) copy-start(f32[256,256]{1,0:T(8,128)} %probe_re.3) | copy-start | bytes 786436
  0.7 16.6 %copy-start.3 = (s32[1,2,12,2]{2,3,1,0:T(2,128)S(1)}, s32[1,2,12,2]{2,3,1,0:T(2,128)}, u32[]{:S(2)}) copy-start(s32[1,2,12,2]{2,3,1,0:T(2,128)} %param.13) | copy-start | bytes 580

commit v7 on v6

--- a/solution.py
+++ b/solution.py
@@ -17,8 +17,7 @@
 ROWS = TR + N
 MESH = pl.DeviceIdType.MESH
 CH = 32
-LAST = 8
-PIECE = TR // 8
+LAST = 6
 EDGE = NTX // 2
 DETOUR = ((1, 0, 0), (2, 0, 1), (3, 1, 0), (3, 1, 1))
 F32 = jnp.float32
@@ -49,7 +48,7 @@
 
 
 def halo_kernel(
-    obj_re, obj_im, amp, reg, amp_out, raw, perm,
+    obj_re, obj_im, amp, reg, amp_out, blank, raw, perm,
     ty_send, ty_recv, up_send, up_recv, diag_send, diag_recv, own_sem, raw_sem,
     relay, detour_send, detour_recv, relay_send,
 ):
@@ -160,6 +159,7 @@
             detour(n).wait_recv()
             onward(n).start()
 
+    blank[...] = jnp.zeros_like(blank)
     for c in raw_copies:
         c.wait()
 
@@ -220,9 +220,10 @@
         out_shape=(
             pltpu.VMEM((2, 3, ROWS, H), F32),
             pltpu.VMEM((SLOTS, N, N), F32),
+            pltpu.VMEM((2, 3, ROWS, H), F32),
         ),
         in_specs=[hbm, hbm, hbm],
-        out_specs=(vmem, vmem),
+        out_specs=(vmem, vmem, vmem),
         scratch_shapes=[
             pltpu.VMEM((2, SLOTS, N, H), F32),
             pltpu.VMEM((N, N), BF16),
@@ -358,11 +359,10 @@
 
 
 def positions_kernel(
-    offsets, counts, reg, probe_re, probe_im, tables, amp, grad, pgrad, win, sp, mid,
+    offsets, counts, reg, probe_re, probe_im, tables, amp, blank, grad, pgrad, win, sp, mid,
 ):
     tx, ty = lax.axis_index("tx"), lax.axis_index("ty")
     here = jnp.maximum(counts[0, ty] - LAST, 0)
-    grad[...] = jnp.zeros_like(grad)
     pgrad[...] = jnp.zeros_like(pgrad)
     pair = pair_of_positions(reg, probe_re, probe_im, tables, amp, win, sp, mid)
 
@@ -383,7 +383,7 @@
     lax.fori_loop(0, (here + 1) // 2, step, 0)
 
 
-def positions(offsets, counts, reg, probe_re, probe_im, tables, amp):
+def positions(offsets, counts, reg, probe_re, probe_im, tables, amp, blank):
     smem = pl.BlockSpec(memory_space=pltpu.SMEM)
     vmem = pl.BlockSpec(memory_space=pltpu.VMEM)
     return pl.pallas_call(
@@ -392,7 +392,8 @@
             pltpu.VMEM((2, 3, ROWS, H), F32),
             pltpu.VMEM((2, 2, N, H), F32),
         ),
-        in_specs=[smem, smem, vmem, vmem, vmem, vmem, vmem],
+        in_specs=[smem, smem] + [vmem] * 6,
+        input_output_aliases={7: 0},
         out_specs=(vmem, vmem),
         scratch_shapes=[
             pltpu.VMEM((2, 2, 2, N, H), F32),
@@ -401,14 +402,14 @@
         ],
         compiler_params=pltpu.CompilerParams(vmem_limit_bytes=20 << 20),
         name="positions",
-    )(offsets, counts, reg, probe_re, probe_im, tables, amp)
+    )(offsets, counts, reg, probe_re, probe_im, tables, amp, blank)
 
 
 def out_kernel(
     offsets, counts, reg, probe_re, probe_im, tables, amp, grad_in, pgrad_in, grad, out_ty, out_up, out_full, out_other,
-    pgrad, placed, win, sp, mid, came_diag, edge, core_in, acc, xy_in, shared,
+    pgrad, placed, win, sp, mid, came_diag, edge, core_in, acc, yz_in, shared,
     ty_send, ty_recv, up_send, up_recv, diag_send, diag_recv,
-    core_send, core_recv, xy_send, xy_recv, z_send, z_recv,
+    core_send, core_recv, yz_send, yz_recv, far_send, far_recv,
 ):
     tx, ty = lax.axis_index("tx"), lax.axis_index("ty")
     up, down = lax.rem(tx + NTX - 1, NTX), lax.rem(tx + 1, NTX)
@@ -420,12 +421,14 @@
         return (((lax.rem(x_, 2) * 8 + z_) * 4 + y_) * 2 + core_, x_ // 2)
 
     core_mate = at(1 - core, y, z, x)
+    z_low, z_high = lax.rem(z, 4), z // 4
     steps = [(i, j) for i in range(4) for j in range(4) if i or j]
     steps.sort(key=lambda s: -(min(s[0], 4 - s[0]) + min(s[1], 4 - s[1])))
-    xy_at = [(lax.rem(y + i, 4), lax.rem(x + j, 4)) for i, j in steps]
-    xy_mates = [at(core, i, z, j) for i, j in xy_at]
-    z_mates = [at(core, y, lax.rem(z + d, 8), x) for d in (4, 3, 5, 2, 6, 1, 7)]
-    greeted = z_mates + xy_mates + [partner, (up, ty), (down, ty), core_mate]
+    yz_at = [(lax.rem(y + i, 4), lax.rem(z_low + j, 4)) for i, j in steps]
+    yz_mates = [at(core, i, z_high * 4 + j, x) for i, j in yz_at]
+    hops = [(1, 2), (1, 1), (1, 3), (1, 0), (0, 2), (0, 1), (0, 3)]
+    far_mates = [at(core, y, lax.rem(z_high + i, 2) * 4 + z_low, lax.rem(x + j, 4)) for i, j in hops]
+    greeted = far_mates + yz_mates + [partner, (up, ty), (down, ty), core_mate]
     barrier = pltpu.get_barrier_semaphore()
     for device in greeted:
         pl.semaphore_signal(barrier, inc=1, device_id=device, device_id_type=MESH)
@@ -499,61 +502,49 @@
         came_diag[...] = jnp.zeros_like(came_diag)
         out_up[...] = jnp.zeros_like(out_up)
 
-    pieces = []
-
-    def send_pieces(count):
-        for _ in range(count):
-            n = (len(pieces) + 4) % 8
-            rows = pl.ds(n * PIECE, PIECE)
-            src = grad.at[:, side, rows] if n >= 4 else edge.at[:, rows]
-            pieces.append(send(src, out_ty.at[:, rows], ty_send.at[n], ty_recv.at[n], partner))
-
-    def start_below():
-        @pl.when(tx < NTX - 1)
-        def _():
-            below.start()
-
-    def add_edge():
-        @pl.when(tx > 0)
-        def _():
-            diag.wait_recv()
-
-        for p in range(2):
-            edge[p] = grad[p, side, pl.ds(0, N)] + came_diag[p]
-
-    send_pieces(2)
+    far_rows = send(
+        grad.at[:, side, pl.ds(N, N)], out_ty.at[:, pl.ds(N, N)], ty_send.at[1], ty_recv.at[1], partner)
     core_copy.wait()
     for t in range(2):
         acc[pl.ds(t * N, N), :] = pgrad[core, t] + core_in[t]
-    xy_copies = [
-        send(acc.at[part(*xy_at[d])], xy_in.at[d], xy_send.at[0, d], xy_recv.at[0, d], xy_mates[d])
+    yz_copies = [
+        send(acc.at[part(*yz_at[d])], yz_in.at[d], yz_send.at[0, d], yz_recv.at[0, d], yz_mates[d])
         for d in range(15)]
-    send_pieces(2)
-    add_edge()
-    for c in xy_copies:
+
+    @pl.when(tx > 0)
+    def _():
+        diag.wait_recv()
+
+    for p in range(2):
+        edge[p] = grad[p, side, pl.ds(0, N)] + came_diag[p]
+    for c in yz_copies:
         c.wait()
-    total = acc[part(y, x), :]
+    total = acc[part(y, z_low), :]
     for d in range(15):
-        total = total + xy_in[d]
-    shared[z] = total
-    z_copies = [
-        send(shared.at[z], shared.at[z], z_send.at[d], z_recv.at[d], z_mates[d]) for d in range(7)]
-    start_below()
-    send_pieces(4)
-    for c in z_copies:
+        total = total + yz_in[d]
+    mine = x * 2 + z_high
+    shared[mine] = total
+    far_copies = [
+        send(shared.at[mine], shared.at[mine], far_send.at[d], far_recv.at[d], far_mates[d]) for d in range(7)]
+    near_rows = send(edge, out_ty.at[:, pl.ds(0, N)], ty_send.at[0], ty_recv.at[0], partner)
+
+    @pl.when(tx < NTX - 1)
+    def _():
+        below.start()
+
+    for c in far_copies:
         c.wait()
     total = shared[0]
     for d in range(1, 8):
         total = total + shared[d]
-    out_full[part(y, x), :] = total * (1.0 / (NTX * 2 * SLOTS))
-    xy_copies = [
-        send(out_full.at[part(y, x)], out_full.at[part(y, x)], xy_send.at[1, d], xy_recv.at[1, d], xy_mates[d])
+    out_full[part(y, z_low), :] = total * (1.0 / (NTX * 2 * SLOTS))
+    yz_copies = [
+        send(out_full.at[part(y, z_low)], out_full.at[part(y, z_low)],
+             yz_send.at[1, d], yz_recv.at[1, d], yz_mates[d])
         for d in range(15)]
-    for c in xy_copies:
+    for c in yz_copies:
         c.wait()
     core_copy = send(out_full, out_other, core_send.at[1], core_recv.at[1], core_mate)
-    for c in pieces:
-        c.wait()
 
     @pl.when(tx < NTX - 1)
     def _():
@@ -564,23 +555,44 @@
     def _():
         below.wait_recv()
 
+    far_rows.wait()
+    near_rows.wait()
     core_copy.wait()
 
 
-def finish_kernel(grad, came_ty, came_up, full, other, out_re, out_im, pout_re, pout_im):
+def finish_kernel(
+    grad, came_ty, came_up, full, other, out_re, out_im, pout_re, pout_im, whole, out_sem, pout_sem,
+):
     core, ty = lax.rem(lax.axis_index("tx"), 2), lax.axis_index("ty")
+
+    def probe_copies(re, im):
+        return [
+            pltpu.make_async_copy(
+                src.at[pl.ds(t * N, N)], dst.at[:, pl.ds(t * H, H)], pout_sem.at[k, t])
+            for k, (src, dst) in enumerate(((re, pout_re), (im, pout_im))) for t in range(2)]
+
+    @pl.when(core == 0)
+    def _():
+        for c in probe_copies(full, other):
+            c.start()
+
+    @pl.when(core == 1)
+    def _():
+        for c in probe_copies(other, full):
+            c.start()
+
+    copies = []
     for p, out in enumerate((out_re, out_im)):
-        for t in range(2):
-            lanes = pl.ds(t * H, H)
-            mine = ty == 1 - t
-            ty_rows = [jnp.where(mine, came_ty[p, pl.ds(h * N, N)], 0.0) for h in range(2)]
-            out[pl.ds(0, N), lanes] = grad[p, ty + t, pl.ds(0, N)] + came_up[p, t] + ty_rows[0]
-            out[pl.ds(N, N), lanes] = grad[p, ty + t, pl.ds(N, N)] + ty_rows[1]
-    for t in range(2):
-        rows, lanes = pl.ds(t * N, N), pl.ds(t * H, H)
-        a, b = full[rows, :], other[rows, :]
-        pout_re[:, lanes] = jnp.where(core == 0, a, b)
-        pout_im[:, lanes] = jnp.where(core == 0, b, a)
+        for h in range(2):
+            rows = pl.ds(h * N, N)
+            for t in range(2):
+                mine = jnp.where(ty == 1 - t, came_ty[p, rows], 0.0)
+                total = grad[p, ty + t, rows] + mine
+                whole[p, rows, pl.ds(t * H, H)] = total + came_up[p, t] if h == 0 else total
+            copies.append(pltpu.make_async_copy(whole.at[p, rows], out.at[rows], out_sem.at[p, h]))
+            copies[-1].start()
+    for c in copies + probe_copies(full, other):
+        c.wait()
 
 
 def gather_out(offsets, counts, reg, probe_re, probe_im, tables, amp, grad, pgrad):
@@ -612,7 +624,7 @@
             pltpu.VMEM((2 * N, H), F32),
             pltpu.VMEM((15, 32, H), F32),
             pltpu.VMEM((8, 32, H), F32),
-            dma((8,)), dma((8,)), dma(()), dma(()), dma(()), dma(()),
+            dma((2,)), dma((2,)), dma(()), dma(()), dma(()), dma(()),
             dma((2,)), dma((2,)), dma((2, 15)), dma((2, 15)), dma((7,)), dma((7,)),
         ],
         compiler_params=pltpu.CompilerParams(
@@ -623,7 +635,8 @@
         finish_kernel,
         out_shape=(tile, tile, patch, patch),
         in_specs=[vmem] * 5,
-        out_specs=(vmem,) * 4,
+        out_specs=(pl.BlockSpec(memory_space=pltpu.HBM),) * 4,
+        scratch_shapes=[pltpu.VMEM((2, TR, N), F32), dma((2, 2)), dma((2, 2))],
         compiler_params=pltpu.CompilerParams(vmem_limit_bytes=20 << 20),
         name="finish",
     )(grad, *came)
@@ -631,9 +644,9 @@
 
 def per_device(obj_re, obj_im, probe_re, probe_im, amplitude, offsets, counts):
     tables = jnp.asarray(half_dft_tables())
-    reg, amp = halo(obj_re, obj_im, amplitude)
+    reg, amp, blank = halo(obj_re, obj_im, amplitude)
     shared = (jnp.swapaxes(offsets, 2, 3), counts, reg, probe_re, probe_im, tables, amp)
-    grad, pgrad = positions(*shared)
+    grad, pgrad = positions(*shared, blank)
     return gather_out(*shared, grad, pgrad)
 
 

time: 70 us -> 65.7 us (0.939)
  Pallas kernels: 69.2 us -> 64.9 us
    pallas_call x1, Pallas kernels: 50.5 us -> 46.5 us  [gather_out(): pl.pallas_call(out_kernel, out_shape=(pltpu.VMEM((2, 3, ROWS, H), F32), j...]
where the time goes in v7:
time: 65.7 us; the launch traced here: 65.6 us
  Pallas kernels  64.9 us (99%)
  between operations  0.74 us (1%)
    pallas_call x1, Pallas kernels, gather_out(): pl.pallas_call(out_kernel, out_shape=(pltpu.VMEM((2, 3, ROWS, H), F32), j...  46.5 us
    pallas_call x1, Pallas kernels, halo(): pl.pallas_call(halo_kernel, out_shape=(pltpu.VMEM((2, 3, ROWS, H), F32),...  16.5 us

profile of v7, /device:TPU:1, one launch (start us, length us, event | category | flops | bytes accessed | tf_op | source)
XLA Modules:
  0.0 65.6 jit_solution(5864716640899716925)
XLA Ops:
  0.6 0.0 copy-start
  0.6 0.0 copy-start.4
  0.7 0.0 copy-start.2
  0.7 0.0 copy-start.1
  0.7 0.0 copy-start.3
  0.7 16.5 %halo.1 = (f32[2,3,768,128]{3,2,1,0:T(8,128)S(1)}, f32[12,256,256]{2,1,0:T(8,128)S(1)}, f32[2,3,768,128]{3,2,1,0:T(8,128)S(1)}) custom-call(f32[512,256]{1,0:T(8,128)} %obj_re.1, f32[512,256]{1,0:T(8,128)} %obj_im.1, f32[1,1,12,256,256]{4,3,2,1,0:T(8,128)} %amp.1), custom_call_target="tpu_custom_call" | custom-call | tf_op jit(solution)/shard_map/halo/pallas_call | solution.py:218
  17.2 0.0 copy-done
  17.3 0.0 copy-done.4
  17.3 0.0 copy-done.2
  17.3 0.0 copy-done.1
  17.3 0.0 copy-done.3
  17.3 0.6 positions.1
  17.9 46.5 %gather_out.1 = (f32[2,3,768,128]{3,2,1,0:T(8,128)S(1)}, f32[2,512,128]{2,1,0:T(8,128)S(1)}, f32[2,2,256,128]{3,2,1,0:T(8,128)S(1)}, f32[512,128]{1,0:T(8,128)S(1)}, f32[512,128]{1,0:T(8,128)S(1)}) custom-call(s32[1,2,2,12]{3,2,1,0:T(2,128)S(1)} %bitcast.2, s32[1,2]{1,0:T(1,128)S(1)} %copy-done.4, f32[2,3,768,128]{3,2,1,0:T(8,128)S(1)} %get-tuple-element.14.reg, ...), custom_call_target="tpu_custom_call" | custom-call | tf_op jit(solution)/shard_map/gather_out/pallas_call | solution.py:604
  64.4 1.3 %finish.1 = (f32[512,256]{1,0:T(8,128)}, f32[512,256]{1,0:T(8,128)}, f32[256,256]{1,0:T(8,128)}, f32[256,256]{1,0:T(8,128)}) custom-call(f32[2,3,768,128]{3,2,1,0:T(8,128)S(1)} %get-tuple-element.19.grad, f32[2,512,128]{2,1,0:T(8,128)S(1)} %get-tuple-element.20.came_ty, f32[2,2,256,128]{3,2,1,0:T(8,128)S(1)} %get-tuple-element.21.came_up, ...), custom_call_target="tpu_custom_call" | custom-call | tf_op jit(solution)/shard_map/finish/pallas_call | solution.py:634
Async XLA Ops:
  0.6 16.6 %copy-start = (bf16[2,4,256,256]{3,2,1,0:T(8,128)(2,1)S(1)}, bf16[2,4,256,256]{3,2,1,0:T(8,128)(2,1)}, u32[]{:S(2)}) copy-start(bf16[2,4,256,256]{3,2,1,0:T(8,128)(2,1)} %constant.2.clone.tables) | copy-start | bytes 3145732
  0.6 16.6 %copy-start.4 = (s32[1,2]{1,0:T(1,128)S(1)}, s32[1,2]{1,0:T(1,128)}, u32[]{:S(2)}) copy-start(s32[1,2]{1,0:T(1,128)} %counts.3) | copy-start | bytes 28
  0.7 16.6 %copy-start.2 = (f32[256,256]{1,0:T(8,128)S(1)}, f32[256,256]{1,0:T(8,128)}, u32[]{:S(2)}) copy-start(f32[256,256]{1,0:T(8,128)} %probe_im.3) | copy-start | bytes 786436
  0.7 16.6 %copy-start.1 = (f32[256,256]{1,0:T(8,128)S(1)}, f32[256,256]{1,0:T(8,128)}, u32[]{:S(2)}) copy-start(f32[256,256]{1,0:T(8,128)} %probe_re.3) | copy-start | bytes 786436
  0.7 16.6 %copy-start.3 = (s32[1,2,12,2]{2,3,1,0:T(2,128)S(1)}, s32[1,2,12,2]{2,3,1,0:T(2,128)}, u32[]{:S(2)}) copy-start(s32[1,2,12,2]{2,3,1,0:T(2,128)} %param.13) | copy-start | bytes 580

commit v8 on v7

--- a/solution.py
+++ b/solution.py
@@ -104,12 +104,12 @@
     for half in range(2):
         for p, obj in enumerate((obj_re, obj_im)):
             rows = pl.ds(half * N, N)
-            c = pltpu.make_async_remote_copy(
+            across[half].append(pltpu.make_async_remote_copy(
                 src_ref=obj.at[rows, pl.ds(edge, H)], dst_ref=reg.at[p, 2 * ty, rows],
                 send_sem=ty_send.at[half, p], recv_sem=ty_recv.at[half, p],
-                device_id=partner, device_id_type=MESH)
-            c.start()
-            across[half].append(c)
+                device_id=partner, device_id_type=MESH))
+    for c in across[0]:
+        c.start()
     objs = (obj_re, obj_im)
     blocks = [(p, t) for p in range(2) for t in range(2)]
 
@@ -152,13 +152,6 @@
         for n in range(4):
             detour(n).start()
 
-    for n in range(4):
-
-        @pl.when(tx == EDGE + 2 * DETOUR[n][0])
-        def _():
-            detour(n).wait_recv()
-            onward(n).start()
-
     blank[...] = jnp.zeros_like(blank)
     for c in raw_copies:
         c.wait()
@@ -171,14 +164,25 @@
         return carry
 
     lax.fori_loop(0, SLOTS // 2, sort_slot, 0)
+    for c in across[0]:
+        c.wait_send()
+    for c in across[1]:
+        c.start()
     for p in range(2):
-        across[0][p].wait()
+        across[0][p].wait_recv()
 
         @pl.when(tx > 0)
         def _():
             diag(p).start()
 
     lax.fori_loop(SLOTS // 2, SLOTS, sort_slot, 0)
+    for n in range(4):
+
+        @pl.when(tx == EDGE + 2 * DETOUR[n][0])
+        def _():
+            detour(n).wait_recv()
+            onward(n).start()
+
 
     for c in own + across[1]:
         c.wait()

time: 65.7 us -> 67.2 us (1.023)
  Pallas kernels: 64.9 us -> 66.3 us
    pallas_call x1, Pallas kernels: 46.5 us -> 47.8 us  [gather_out(): pl.pallas_call(out_kernel, out_shape=(pltpu.VMEM((2, 3, ROWS, H), F32), j...]
where the time goes in v8:
time: 67.2 us; the launch traced here: 67.1 us
  Pallas kernels  66.3 us (99%)
  between operations  0.74 us (1%)
    pallas_call x1, Pallas kernels, gather_out(): pl.pallas_call(out_kernel, out_shape=(pltpu.VMEM((2, 3, ROWS, H), F32), j...  47.8 us
    pallas_call x1, Pallas kernels, halo(): pl.pallas_call(halo_kernel, out_shape=(pltpu.VMEM((2, 3, ROWS, H), F32),...  16.7 us

profile of v8, /device:TPU:1, one launch (start us, length us, event | category | flops | bytes accessed | tf_op | source)
XLA Modules:
  0.0 67.1 jit_solution(639646296128371281)
XLA Ops:
  0.6 0.0 copy-start
  0.6 0.0 copy-start.4
  0.7 0.0 copy-start.2
  0.7 0.0 copy-start.1
  0.7 0.0 copy-start.3
  0.7 16.7 %halo.1 = (f32[2,3,768,128]{3,2,1,0:T(8,128)S(1)}, f32[12,256,256]{2,1,0:T(8,128)S(1)}, f32[2,3,768,128]{3,2,1,0:T(8,128)S(1)}) custom-call(f32[512,256]{1,0:T(8,128)} %obj_re.1, f32[512,256]{1,0:T(8,128)} %obj_im.1, f32[1,1,12,256,256]{4,3,2,1,0:T(8,128)} %amp.1), custom_call_target="tpu_custom_call" | custom-call | tf_op jit(solution)/shard_map/halo/pallas_call | solution.py:222
  17.3 0.0 copy-done
  17.4 0.0 copy-done.4
  17.4 0.0 copy-done.2
  17.4 0.0 copy-done.1
  17.4 0.0 copy-done.3
  17.4 0.6 positions.1
  18.0 47.8 %gather_out.1 = (f32[2,3,768,128]{3,2,1,0:T(8,128)S(1)}, f32[2,512,128]{2,1,0:T(8,128)S(1)}, f32[2,2,256,128]{3,2,1,0:T(8,128)S(1)}, f32[512,128]{1,0:T(8,128)S(1)}, f32[512,128]{1,0:T(8,128)S(1)}) custom-call(s32[1,2,2,12]{3,2,1,0:T(2,128)S(1)} %bitcast.2, s32[1,2]{1,0:T(1,128)S(1)} %copy-done.4, f32[2,3,768,128]{3,2,1,0:T(8,128)S(1)} %get-tuple-element.14.reg, ...), custom_call_target="tpu_custom_call" | custom-call | tf_op jit(solution)/shard_map/gather_out/pallas_call | solution.py:608
  65.8 1.3 %finish.1 = (f32[512,256]{1,0:T(8,128)}, f32[512,256]{1,0:T(8,128)}, f32[256,256]{1,0:T(8,128)}, f32[256,256]{1,0:T(8,128)}) custom-call(f32[2,3,768,128]{3,2,1,0:T(8,128)S(1)} %get-tuple-element.19.grad, f32[2,512,128]{2,1,0:T(8,128)S(1)} %get-tuple-element.20.came_ty, f32[2,2,256,128]{3,2,1,0:T(8,128)S(1)} %get-tuple-element.21.came_up, ...), custom_call_target="tpu_custom_call" | custom-call | tf_op jit(solution)/shard_map/finish/pallas_call | solution.py:638
Async XLA Ops:
  0.6 16.7 %copy-start = (bf16[2,4,256,256]{3,2,1,0:T(8,128)(2,1)S(1)}, bf16[2,4,256,256]{3,2,1,0:T(8,128)(2,1)}, u32[]{:S(2)}) copy-start(bf16[2,4,256,256]{3,2,1,0:T(8,128)(2,1)} %constant.2.clone.tables) | copy-start | bytes 3145732
  0.6 16.7 %copy-start.4 = (s32[1,2]{1,0:T(1,128)S(1)}, s32[1,2]{1,0:T(1,128)}, u32[]{:S(2)}) copy-start(s32[1,2]{1,0:T(1,128)} %counts.3) | copy-start | bytes 28
  0.7 16.7 %copy-start.2 = (f32[256,256]{1,0:T(8,128)S(1)}, f32[256,256]{1,0:T(8,128)}, u32[]{:S(2)}) copy-start(f32[256,256]{1,0:T(8,128)} %probe_im.3) | copy-start | bytes 786436
  0.7 16.7 %copy-start.1 = (f32[256,256]{1,0:T(8,128)S(1)}, f32[256,256]{1,0:T(8,128)}, u32[]{:S(2)}) copy-start(f32[256,256]{1,0:T(8,128)} %probe_re.3) | copy-start | bytes 786436
  0.7 16.7 %copy-start.3 = (s32[1,2,12,2]{2,3,1,0:T(2,128)S(1)}, s32[1,2,12,2]{2,3,1,0:T(2,128)}, u32[]{:S(2)}) copy-start(s32[1,2,12,2]{2,3,1,0:T(2,128)} %param.13) | copy-start | bytes 580

commit v9 on v8

--- a/solution.py
+++ b/solution.py
@@ -514,13 +514,6 @@
     yz_copies = [
         send(acc.at[part(*yz_at[d])], yz_in.at[d], yz_send.at[0, d], yz_recv.at[0, d], yz_mates[d])
         for d in range(15)]
-
-    @pl.when(tx > 0)
-    def _():
-        diag.wait_recv()
-
-    for p in range(2):
-        edge[p] = grad[p, side, pl.ds(0, N)] + came_diag[p]
     for c in yz_copies:
         c.wait()
     total = acc[part(y, z_low), :]
@@ -530,6 +523,13 @@
     shared[mine] = total
     far_copies = [
         send(shared.at[mine], shared.at[mine], far_send.at[d], far_recv.at[d], far_mates[d]) for d in range(7)]
+
+    @pl.when(tx > 0)
+    def _():
+        diag.wait_recv()
+
+    for p in range(2):
+        edge[p] = grad[p, side, pl.ds(0, N)] + came_diag[p]
     near_rows = send(edge, out_ty.at[:, pl.ds(0, N)], ty_send.at[0], ty_recv.at[0], partner)
 
     @pl.when(tx < NTX - 1)

time: 67.2 us -> 66.5 us (0.990)
  Pallas kernels: 66.3 us -> 65.3 us
    pallas_call x1, Pallas kernels: 47.8 us -> 44.2 us  [gather_out(): pl.pallas_call(out_kernel, out_shape=(pltpu.VMEM((2, 3, ROWS, H), F32), j...]
    pallas_call x1, Pallas kernels: 0.61 us -> 3.22 us  [positions(): pl.pallas_call(positions_kernel, out_shape=(pltpu.VMEM((2, 3, ROWS, H), F...]
where the time goes in v9:
time: 66.5 us; the launch traced here: 66.1 us
  Pallas kernels  65.3 us (98%)
  between operations  0.74 us (1%)
    pallas_call x1, Pallas kernels, gather_out(): pl.pallas_call(out_kernel, out_shape=(pltpu.VMEM((2, 3, ROWS, H), F32), j...  44.2 us
    pallas_call x1, Pallas kernels, halo(): pl.pallas_call(halo_kernel, out_shape=(pltpu.VMEM((2, 3, ROWS, H), F32),...  16.7 us
    pallas_call x1, Pallas kernels, positions(): pl.pallas_call(positions_kernel, out_shape=(pltpu.VMEM((2, 3, ROWS, H), F...  3.22 us

profile of v9, /device:TPU:1, one launch (start us, length us, event | category | flops | bytes accessed | tf_op | source)
XLA Modules:
  0.0 66.1 jit_solution(3020677808221990243)
XLA Ops:
  0.6 0.0 copy-start
  0.6 0.0 copy-start.4
  0.7 0.0 copy-start.2
  0.7 0.0 copy-start.1
  0.7 0.0 copy-start.3
  0.7 16.7 %halo.1 = (f32[2,3,768,128]{3,2,1,0:T(8,128)S(1)}, f32[12,256,256]{2,1,0:T(8,128)S(1)}, f32[2,3,768,128]{3,2,1,0:T(8,128)S(1)}) custom-call(f32[512,256]{1,0:T(8,128)} %obj_re.1, f32[512,256]{1,0:T(8,128)} %obj_im.1, f32[1,1,12,256,256]{4,3,2,1,0:T(8,128)} %amp.1), custom_call_target="tpu_custom_call" | custom-call | tf_op jit(solution)/shard_map/halo/pallas_call | solution.py:222
  17.3 0.0 copy-done
  17.4 0.0 copy-done.4
  17.4 0.0 copy-done.2
  17.4 0.0 copy-done.1
  17.4 0.0 copy-done.3
  17.4 3.2 %positions.1 = (f32[2,3,768,128]{3,2,1,0:T(8,128)S(1)}, f32[2,2,256,128]{3,2,1,0:T(8,128)S(1)}) custom-call(s32[1,2,2,12]{3,2,1,0:T(2,128)S(1)} %bitcast.1, s32[1,2]{1,0:T(1,128)S(1)} %copy-done.4, f32[2,3,768,128]{3,2,1,0:T(8,128)S(1)} %get-tuple-element.14.reg, f32[256,256]{1,0:T(8,128)S(1)} %copy-done.1, ...), custom_call_target="tpu_custom_call", output_to_operand_aliasing={{0}: (7, {})} | custom-call | tf_op jit(solution)/shard_map/positions/pallas_call | solution.py:393
  20.6 44.2 %gather_out.1 = (f32[2,3,768,128]{3,2,1,0:T(8,128)S(1)}, f32[2,512,128]{2,1,0:T(8,128)S(1)}, f32[2,2,256,128]{3,2,1,0:T(8,128)S(1)}, f32[512,128]{1,0:T(8,128)S(1)}, f32[512,128]{1,0:T(8,128)S(1)}) custom-call(s32[1,2,2,12]{3,2,1,0:T(2,128)S(1)} %bitcast.2, s32[1,2]{1,0:T(1,128)S(1)} %copy-done.4, f32[2,3,768,128]{3,2,1,0:T(8,128)S(1)} %get-tuple-element.14.reg, ...), custom_call_target="tpu_custom_call" | custom-call | tf_op jit(solution)/shard_map/gather_out/pallas_call | solution.py:608
  64.9 1.3 %finish.1 = (f32[512,256]{1,0:T(8,128)}, f32[512,256]{1,0:T(8,128)}, f32[256,256]{1,0:T(8,128)}, f32[256,256]{1,0:T(8,128)}) custom-call(f32[2,3,768,128]{3,2,1,0:T(8,128)S(1)} %get-tuple-element.19.grad, f32[2,512,128]{2,1,0:T(8,128)S(1)} %get-tuple-element.20.came_ty, f32[2,2,256,128]{3,2,1,0:T(8,128)S(1)} %get-tuple-element.21.came_up, ...), custom_call_target="tpu_custom_call" | custom-call | tf_op jit(solution)/shard_map/finish/pallas_call | solution.py:638
Async XLA Ops:
  0.6 16.7 %copy-start = (bf16[2,4,256,256]{3,2,1,0:T(8,128)(2,1)S(1)}, bf16[2,4,256,256]{3,2,1,0:T(8,128)(2,1)}, u32[]{:S(2)}) copy-start(bf16[2,4,256,256]{3,2,1,0:T(8,128)(2,1)} %constant.2.clone.tables) | copy-start | bytes 3145732
  0.6 16.7 %copy-start.4 = (s32[1,2]{1,0:T(1,128)S(1)}, s32[1,2]{1,0:T(1,128)}, u32[]{:S(2)}) copy-start(s32[1,2]{1,0:T(1,128)} %counts.3) | copy-start | bytes 28
  0.7 16.7 %copy-start.2 = (f32[256,256]{1,0:T(8,128)S(1)}, f32[256,256]{1,0:T(8,128)}, u32[]{:S(2)}) copy-start(f32[256,256]{1,0:T(8,128)} %probe_im.3) | copy-start | bytes 786436
  0.7 16.7 %copy-start.1 = (f32[256,256]{1,0:T(8,128)S(1)}, f32[256,256]{1,0:T(8,128)}, u32[]{:S(2)}) copy-start(f32[256,256]{1,0:T(8,128)} %probe_re.3) | copy-start | bytes 786436
  0.7 16.7 %copy-start.3 = (s32[1,2,12,2]{2,3,1,0:T(2,128)S(1)}, s32[1,2,12,2]{2,3,1,0:T(2,128)}, u32[]{:S(2)}) copy-start(s32[1,2,12,2]{2,3,1,0:T(2,128)} %param.13) | copy-start | bytes 580
